TPU v7x, 128 devices: a whole 4x4x4 slice. The times are simulated.
128 devices in a mesh: leaf: 32 (over y, z, core), slab: 4 (over x).
Axes of the slice: x: 4, y: 4, z: 4, core: 2. Of those that a mesh axis runs over, the one named last changes fastest.
Arguments:
- sources: bfloat16 [8192, 16, 256], P(('slab', 'leaf')), may hold values from -6 to 6
- source_basis: bfloat16 [8192, 64, 256], P(('slab', 'leaf')), may hold values from -0.375 to 0.375
- target_basis: bfloat16 [8192, 64, 256], P(('slab', 'leaf')), may hold values from -0.75 to 0.75
- up_leaf: float32 [8192, 64, 64], P(('slab', 'leaf')), may hold values from -0.375 to 0.375
- down_leaf: float32 [8192, 64, 64], P(('slab', 'leaf')), may hold values from -0.75 to 0.75
- up_section: float32 [2048, 64, 64], P(('slab', 'leaf')), may hold values from -0.09375 to 0.09375
- down_section: float32 [2048, 64, 64], P(('slab', 'leaf')), may hold values from -0.75 to 0.75
- section_coupling: float32 [2048, 8, 64, 64], P(('slab', 'leaf')), may hold values from -0.25 to 0.25
- top_coupling: float32 [32, 8, 64, 64], P('slab'), may hold values from -0.25 to 0.25
- near_blocks: bfloat16 [9, 256, 256], replicated, may hold values from -0.125 to 0.125
- leaf_parent: int32 [8192], P(('slab', 'leaf')), may hold values from 0 to 2047, as said below
- near_list: int32 [8192, 9], P(('slab', 'leaf')), may hold values from 0 to 8191, as said below
- section_list: int32 [2048, 8], P(('slab', 'leaf')), may hold values from 0 to 2047, as said below
- top_list: int32 [32, 8], P('slab'), may hold values from 0 to 31, as said below
Outputs:
- potential: bfloat16 [8192, 16, 256], P(('slab', 'leaf'))
Inputs may be any that keep to these rules, and one draw needn't show every extreme that they name: `leaf_parent`: the section box is held by the same device as the leaf box; each section box is named by exactly 4 leaf boxes. `near_list`: let leaf box b be held by device (s, i). Its 9 entries name boxes on the nine devices (s + a mod 4, i + c mod 32) for a, c in -1, 0, 1, one entry on each. `section_list`: each entry names a section box on the device one step lower or one step higher along leaf (cyclically) in the same slab; every section box has entries on both. `top_list`: no top box is coupled to itself.
All inputs are finite; a program needn't handle non-finite values.
Results may differ from a plain program's by a relative error of at most 0.0046.
Values may be sent and summed in bfloat16 or wider, within the bound.
No kernel may reach another device: no remote copies, remote signals or barrier semaphores. Data moves between devices by JAX's collectives and lax.ppermute only.
A program may use at most 128 MiB of HBM per device.

v0:
```python
import jax
import jax.numpy as jnp
from jax import lax
from jax.sharding import PartitionSpec as P

GROUP = 4


def padded_2(cells, sides, width):
    for axis, dim in sides:
        count = lax.axis_size(axis)
        head = lax.slice_in_dim(cells, 0, width, axis=dim)
        tail = lax.slice_in_dim(cells, cells.shape[dim] - width, cells.shape[dim], axis=dim)
        cells = jnp.concatenate(
            [
                lax.ppermute(tail, axis, [(i, (i + 1) % count) for i in range(count)]),
                cells,
                lax.ppermute(head, axis, [((i + 1) % count, i) for i in range(count)]),
            ],
            axis=dim,
        )
    return cells


def shards(
    sources,
    source_basis,
    target_basis,
    up_leaf,
    down_leaf,
    up_section,
    down_section,
    section_coupling,
    top_coupling,
    near_blocks,
    leaf_parent,
    near_list,
    section_list,
    top_list,
):
    highest = lax.Precision.HIGHEST
    leaf_count = sources.shape[0]
    section_count = up_section.shape[0]
    rhs_count = sources.shape[1]
    rank = source_basis.shape[1]
    leaves = lax.axis_size("leaf")
    slabs = lax.axis_size("slab")
    my_leaf = lax.axis_index("leaf")
    my_slab = lax.axis_index("slab")
    leaf_moments = jnp.einsum(
        "brp,bkp->brk", sources, source_basis, preferred_element_type=jnp.float32
    )
    lifted = jnp.einsum("brk,bkl->brl", leaf_moments, up_leaf, precision=highest)
    local_parent = leaf_parent % section_count
    parent_table = (
        local_parent[:, None] == jnp.arange(section_count, dtype=jnp.int32)[None, :]
    ).astype(jnp.float32)
    section_moments = jnp.einsum("bq,brl->qrl", parent_table, lifted, precision=highest)
    partial_top = jnp.einsum("qrk,qkl->rl", section_moments, up_section, precision=highest)
    pieces = lax.all_gather(partial_top[None], ("slab", "leaf"), axis=0, tiled=True)
    top_moments = pieces.reshape(-1, GROUP, rhs_count, rank).sum(axis=1)
    my_top = my_leaf // GROUP
    links = lax.dynamic_index_in_dim(top_list, my_top, 0, keepdims=False)
    couplers = lax.dynamic_index_in_dim(top_coupling, my_top, 0, keepdims=False)
    top_locals = jnp.einsum("jrk,jkl->rl", top_moments[links], couplers, precision=highest)
    beside = padded_2(section_moments, (("leaf", 0),), section_count)
    side_leaf = section_list // section_count % leaves
    side_slot = (side_leaf - my_leaf + 1) % leaves * section_count + section_list % section_count
    coupled = beside[side_slot]
    section_locals = jnp.einsum("rk,qkl->qrl", top_locals, down_section, precision=highest)
    section_locals = section_locals + jnp.einsum(
        "qjrk,qjkl->qrl", coupled, section_coupling, precision=highest
    )
    inherited = jnp.einsum("bq,qrk->brk", parent_table, section_locals, precision=highest)
    leaf_locals = jnp.einsum("brk,bkl->brl", inherited, down_leaf, precision=highest).astype(
        jnp.bfloat16
    )
    far_field = jnp.einsum(
        "brk,bkp->brp", leaf_locals, target_basis, preferred_element_type=jnp.float32
    )
    padded = padded_2(sources[None, None], (("slab", 0), ("leaf", 1)), 1)
    flat_sources = padded.reshape((9 * leaf_count,) + sources.shape[1:])
    owner = near_list // leaf_count
    rel_slab = (owner // leaves - my_slab + 1) % slabs
    rel_leaf = (owner % leaves - my_leaf + 1) % leaves
    near_slot = (rel_slab * 3 + rel_leaf) * leaf_count + near_list % leaf_count
    gathered = flat_sources[near_slot]
    near_field = jnp.einsum(
        "bjrp,jpq->brq", gathered, near_blocks, preferred_element_type=jnp.float32
    )
    return (far_field + near_field).astype(jnp.bfloat16)


def solution(mesh):
    in_specs = (
        P(("slab", "leaf"), None, None),
        P(("slab", "leaf"), None, None),
        P(("slab", "leaf"), None, None),
        P(("slab", "leaf"), None, None),
        P(("slab", "leaf"), None, None),
        P(("slab", "leaf"), None, None),
        P(("slab", "leaf"), None, None),
        P(("slab", "leaf"), None, None, None),
        P("slab", None, None, None),
        P(),
        P(("slab", "leaf")),
        P(("slab", "leaf"), None),
        P(("slab", "leaf"), None),
        P("slab", None),
    )
    out_specs = P(("slab", "leaf"), None, None)
    return jax.shard_map(shards, mesh=mesh, in_specs=in_specs, out_specs=out_specs, check_vma=False)
```

profile of v0, /device:TPU:0, one launch (start us, length us, event | category | flops | bytes accessed | tf_op | source)
XLA Modules:
  0.0 109.2 jit_solution(4674781474692300734)
XLA Ops:
  0.0 0.8 and_select_fusion
  0.8 2.5 %fusion.41 = f32[64,16,64]{2,1,0:T(8,128)S(1)} fusion(bf16[64,16,256]{2,1,0:T(8,128)(2,1)} %param.14, bf16[64,64,256]{2,1,0:T(8,128)(2,1)} %param.15), kind=kOutput, calls=%fused_computation.89 | convolution fusion | flops 33554432 | bytes 2883584 | tf_op jit(solution)/shard_map/brp,bkp->brk/dot_general | solution.py:50
  3.4 2.0 %fusion.42 = f32[64,16,64]{2,1,0:T(8,128)S(1)} fusion(f32[64,16,64]{2,1,0:T(8,128)S(1)} %fusion.41, f32[64,64,64]{2,1,0:T(8,128)S(1)} %copy-done.2), kind=kOutput, calls=%fused_computation.90 | convolution fusion | flops 50331648 | bytes 1572864 | tf_op jit(solution)/shard_map/brk,bkl->brl/dot_general | solution.py:53
  5.3 0.4 fusion.4
  5.8 6.1 %collective-permute-start.1 = (f32[16,16,64]{2,0,1:T(8,128)S(1)}, f32[16,16,64]{2,0,1:T(8,128)}, u32[]{:S(2)}, u32[]{:S(2)}) collective-permute-start(f32[16,16,64]{2,0,1:T(8,128)S(1)} %fusion.4), channel_id=1, source_target_pairs={{4,0},{8,4},{12,8},{16,12},{20,16},{24,20},{28,24},{32,28},{36,32}... | collective-permute-start | bytes 196616 | tf_op jit(solution)/shard_map/ppermute | solution.py:18
  11.8 2.8 %collective-permute-start.3 = (bf16[1,1,64,16,256]{4,3,2,1,0:T(8,128)(2,1)S(1)}, bf16[1,1,64,16,256]{4,3,2,1,0:T(8,128)(2,1)S(1)}, u32[]{:S(2)}, u32[]{:S(2)}) collective-permute-start(bf16[1,1,64,16,256]{4,3,2,1,0:T(8,128)(2,1)S(1)} %bitcast.53), channel_id=1, source_target_pairs={{1,0},{2,1},{3,2},{0,3},{5,4},{6,5},{7,6},{4,7},{9,8},{10,9},{11,1... | collective-permute-start | bytes 1572872 | tf_op jit(solution)/shard_map/ppermute | solution.py:18
  14.6 1.4 %convolution_bitcast_fusion.1 = f32[16,64]{1,0:T(8,128)S(1)} fusion(f32[16,64,64]{2,1,0:T(8,128)} %param.19, f32[16,16,64]{2,0,1:T(8,128)S(1)} %fusion.4), kind=kOutput, calls=%fused_computation.10 | convolution fusion | flops 12582912 | bytes 331776 | tf_op jit(solution)/shard_map/qrk,qkl->rl/dot_general | solution.py:59
  16.1 41.1 %all-gather = f32[2048,64]{1,0:T(8,128)} all-gather(f32[16,64]{1,0:T(8,128)S(1)} %convolution_bitcast_fusion.1), channel_id=2, replica_groups=mesh['leaf'=32,'slab'=4] {'slab','leaf'}, dimensions={0}, use_global_device_ids=true | all-gather | bytes 528384 | tf_op jit(solution)/shard_map/all_gather | solution.py:60
  57.1 1.2 %fusion.39 = s32[8]{0:T(128)} fusion(s32[8,8]{1,0:T(8,128)} %param.27, s32[]{:T(128)S(6)} %select_n.80), kind=kLoop, calls=%fused_computation.87 | loop fusion | flops 24 | bytes 68 | tf_op jit(solution)/shard_map/select_n | solution.py:65
  58.4 1.3 %reduce_sum.9 = f32[32,16,64]{2,1,0:T(8,128)S(1)} reduce(f32[32,4,16,64]{3,2,1,0:T(8,128)} %bitcast.57, f32[]{:T(128)} %constant.132.clone.1), dimensions={1}, to_apply=%region_0.1 | reduce | flops 98304 | bytes 655364 | tf_op jit(solution)/shard_map/reduce_sum | solution.py:61
  59.7 0.7 pad_clamp_fusion.2
  60.4 1.2 %gather_fusion = f32[8,16,64]{2,1,0:T(8,128)} fusion(f32[32,16,64]{2,1,0:T(8,128)S(1)} %reduce_sum.9, s32[1024]{0:T(1024)S(1)} %pad_clamp_fusion.2), kind=kCustom, calls=%fused_computation | custom fusion | bytes 65568 | tf_op jit(solution)/shard_map/gather | solution.py:65
  61.6 1.3 %fusion.6 = f32[16,64,1]{1,0,2:T(8,128)S(1)} fusion(f32[8,16,64]{2,1,0:T(8,128)} %gather_fusion, f32[8,8,64,64]{3,2,1,0:T(8,128)} %param.22, s32[]{:T(128)S(6)} %select_n.80), kind=kOutput, calls=%fused_computation.15 | convolution fusion | flops 6291456 | bytes 331780 | tf_op jit(solution)/shard_map/jrk,jkl->rl/dot_general | solution.py:65
  62.8 2.1 %fusion.43 = f32[16,16,64]{2,0,1:T(8,128)} fusion(f32[16,64,1]{1,0,2:T(8,128)S(1)} %fusion.6, f32[16,64,64]{2,1,0:T(8,128)} %param.20), kind=kOutput, calls=%fused_computation.91 | convolution fusion | flops 12582912 | bytes 331776 | tf_op jit(solution)/shard_map/rk,qkl->qrl/dot_general | solution.py:70
  64.9 2.4 %pad_maximum_fusion.1 = bf16[3,1,64,16,256]{4,3,2,1,0:T(8,128)(2,1)} fusion(bf16[1,1,64,16,256]{4,3,2,1,0:T(8,128)(2,1)S(1)} %collective-permute-done.3, bf16[1,1,64,16,256]{4,3,2,1,0:T(8,128)(2,1)S(1)} %bitcast.55, bf16[1,1,64,16,256]{4,3,2,1,0:T(8,128)(2,1)} %collective-permute-done.2), kind=kLoop, calls=%fused_computation.4 | loop fusion | flops 1572864 | bytes 3145728 | tf_op jit(solution)/shard_map/concatenate | solution.py:14
  67.3 2.6 %collective-permute-start.5 = (bf16[3,1,64,16,256]{4,3,2,1,0:T(8,128)(2,1)}, bf16[3,1,64,16,256]{4,3,2,1,0:T(8,128)(2,1)}, u32[]{:S(2)}, u32[]{:S(2)}) collective-permute-start(bf16[3,1,64,16,256]{4,3,2,1,0:T(8,128)(2,1)} %pad_maximum_fusion.1), channel_id=1, source_target_pairs={{4,0},{8,4},{12,8},{16,12},{20,16},{24,20},{28,24},{32,28},{36,32}... | collective-permute-start | bytes 4718600 | tf_op jit(solution)/shard_map/ppermute | solution.py:18
  70.0 0.1 copy.18
  70.0 0.1 reshape.47
  70.1 0.1 copy.20
  70.2 0.1 reshape.55
  70.4 1.0 pad_maximum_fusion.2
  71.4 0.1 copy.19
  71.6 1.7 %gather_fusion.1 = f32[128,16,64]{2,1,0:T(8,128)} fusion(f32[48,16,64]{2,1,0:T(8,128)S(1)} %copy.19, s32[1024]{0:T(1024)S(1)} %pad_clamp_fusion.1), kind=kCustom, calls=%fused_computation.1 | custom fusion | bytes 1049088 | tf_op jit(solution)/shard_map/gather | solution.py:69
  73.3 4.9 %fusion.44 = f32[16,16,64,1]{2,1,3,0:T(8,128)S(1)} fusion(f32[16,8,16,64]{3,2,1,0:T(8,128)} %bitcast.58, f32[16,8,64,64]{3,2,1,0:T(8,128)} %param.21), kind=kOutput, calls=%fused_computation.92 | convolution fusion | flops 100663296 | bytes 2686976 | tf_op jit(solution)/shard_map/qjrk,qjkl->qrl/dot_general | solution.py:71
  78.2 0.4 fusion.9
  78.7 2.2 %convolution_convert_fusion = bf16[64,16,64]{2,1,0:T(8,128)(2,1)S(1)} fusion(f32[64,64,64]{2,1,0:T(8,128)S(1)} %copy-done.3, f32[64,16,64]{2,0,1:T(8,128)S(1)} %fusion.9), kind=kOutput, calls=%fused_computation.8 | convolution fusion | flops 50397184 | bytes 1441792 | tf_op jit(solution)/shard_map/brk,bkl->brl/dot_general | solution.py:75
  80.9 1.4 %fusion.45 = f32[64,16,256]{2,1,0:T(8,128)} fusion(bf16[64,16,64]{2,1,0:T(8,128)(2,1)S(1)} %convolution_convert_fusion, bf16[64,64,256]{2,1,0:T(8,128)(2,1)S(1)} %copy-done), kind=kOutput, calls=%fused_computation.93 | convolution fusion | flops 33554432 | bytes 3276800 | tf_op jit(solution)/shard_map/brk,bkp->brp/dot_general | solution.py:78
  82.3 5.9 %collective-permute-done.5 = bf16[3,1,64,16,256]{4,3,2,1,0:T(8,128)(2,1)} collective-permute-done((bf16[3,1,64,16,256]{4,3,2,1,0:T(8,128)(2,1)}, bf16[3,1,64,16,256]{4,3,2,1,0:T(8,128)(2,1)}, u32[]{:S(2)}, u32[]{:S(2)}) %collective-permute-start.5) | collective-permute-done | bytes 1572896 | tf_op jit(solution)/shard_map/ppermute | solution.py:18
  88.2 5.2 %collective-permute-done.4 = bf16[3,1,64,16,256]{4,3,2,1,0:T(8,128)(2,1)} collective-permute-done((bf16[3,1,64,16,256]{4,3,2,1,0:T(8,128)(2,1)}, bf16[3,1,64,16,256]{4,3,2,1,0:T(8,128)(2,1)}, u32[]{:S(2)}, u32[]{:S(2)}) %collective-permute-start.4) | collective-permute-done | bytes 1572896 | tf_op jit(solution)/shard_map/ppermute | solution.py:16
  93.4 3.8 %pad_maximum_fusion = bf16[3,3,64,16,256]{4,3,2,1,0:T(8,128)(2,1)} fusion(bf16[3,1,64,16,256]{4,3,2,1,0:T(8,128)(2,1)} %collective-permute-done.5, bf16[1,1,64,16,256]{4,3,2,1,0:T(8,128)(2,1)S(1)} %collective-permute-done.3, bf16[1,1,64,16,256]{4,3,2,1,0:T(8,128)(2,1)S(1)} %bitcast.56, bf16[1,1,64,16,256]{4,3,2,1,0:T(8,128)(2,1)} %collective-permute-done.2, ...), kind=kLoop, calls=%fused_computation.3 | loop fusion | flops 9437184 | bytes 9437184 | tf_op jit(solution)/shard_map/concatenate | solution.py:14
  97.2 6.9 %gather_fusion.2 = bf16[576,16,256]{2,1,0:T(8,128)(2,1)} fusion(bf16[576,16,256]{2,1,0:T(8,128)(2,1)} %bitcast.51, s32[1024]{0:T(1024)S(1)} %pad_clamp_fusion), kind=kCustom, calls=%fused_computation.2 | custom fusion | bytes 9439488 | tf_op jit(solution)/shard_map/gather | solution.py:87
  104.1 5.1 %fusion.1 = bf16[64,16,256]{2,1,0:T(8,128)(2,1)} fusion(f32[64,16,256]{2,1,0:T(8,128)} %fusion.45, bf16[64,9,16,256]{3,2,1,0:T(8,128)(2,1)} %bitcast.52, bf16[9,256,256]{2,1,0:T(8,128)(2,1)} %param.23), kind=kOutput, calls=%fused_computation.7 | convolution fusion | flops 1208483840 | bytes 7471104 | tf_op jit(solution)/shard_map/bjrp,jpq->brq/dot_general | solution.py:88
  (25 shorter events, 0.1 us)
Async XLA Ops:
  0.0 80.9 %copy-start = (bf16[64,64,256]{2,1,0:T(8,128)(2,1)S(1)}, bf16[64,64,256]{2,1,0:T(8,128)(2,1)}, u32[]{:S(2)}) copy-start(bf16[64,64,256]{2,1,0:T(8,128)(2,1)} %param.16) | copy-start | bytes 6291460
  0.0 3.3 %copy-start.2 = (f32[64,64,64]{2,1,0:T(8,128)S(1)}, f32[64,64,64]{2,1,0:T(8,128)}, u32[]{:S(2)}) copy-start(f32[64,64,64]{2,1,0:T(8,128)} %param.17) | copy-start | bytes 3145732
  3.3 8.5 %copy-start.1 = (bf16[64,16,256]{2,1,0:T(8,128)(2,1)S(1)}, bf16[64,16,256]{2,1,0:T(8,128)(2,1)}, u32[]{:S(2)}) copy-start(bf16[64,16,256]{2,1,0:T(8,128)(2,1)} %param.14) | copy-start | bytes 1572868
  3.3 55.0 %copy-start.5 = (s32[64,9]{0,1:T(8,128)S(1)}, s32[64,9]{0,1:T(8,128)}, u32[]{:S(2)}) copy-start(s32[64,9]{0,1:T(8,128)} %param.25) | copy-start | bytes 6916
  5.8 64.6 %collective-permute-start.1 = (f32[16,16,64]{2,0,1:T(8,128)S(1)}, f32[16,16,64]{2,0,1:T(8,128)}, u32[]{:S(2)}, u32[]{:S(2)}) collective-permute-start(f32[16,16,64]{2,0,1:T(8,128)S(1)} %fusion.4), channel_id=1, source_target_pairs={{4,0},{8,4},{12,8},{16,12},{20,16},{24,20},{28,24},{32,28},{36,32}... | collective-permute-start | bytes 196616 | tf_op jit(solution)/shard_map/ppermute | solution.py:18
  11.8 58.6 %collective-permute-start = (f32[16,16,64]{2,0,1:T(8,128)S(1)}, f32[16,16,64]{2,0,1:T(8,128)}, u32[]{:S(2)}, u32[]{:S(2)}) collective-permute-start(f32[16,16,64]{2,0,1:T(8,128)S(1)} %fusion.4), channel_id=1, source_target_pairs={{0,4},{4,8},{8,12},{12,16},{16,20},{20,24},{24,28},{28,32},{32,36}... | collective-permute-start | bytes 196616 | tf_op jit(solution)/shard_map/ppermute | solution.py:16
  11.8 53.1 %collective-permute-start.3 = (bf16[1,1,64,16,256]{4,3,2,1,0:T(8,128)(2,1)S(1)}, bf16[1,1,64,16,256]{4,3,2,1,0:T(8,128)(2,1)S(1)}, u32[]{:S(2)}, u32[]{:S(2)}) collective-permute-start(bf16[1,1,64,16,256]{4,3,2,1,0:T(8,128)(2,1)S(1)} %bitcast.53), channel_id=1, source_target_pairs={{1,0},{2,1},{3,2},{0,3},{5,4},{6,5},{7,6},{4,7},{9,8},{10,9},{11,1... | collective-permute-start | bytes 1572872 | tf_op jit(solution)/shard_map/ppermute | solution.py:18
  14.6 50.3 %collective-permute-start.2 = (bf16[1,1,64,16,256]{4,3,2,1,0:T(8,128)(2,1)S(1)}, bf16[1,1,64,16,256]{4,3,2,1,0:T(8,128)(2,1)}, u32[]{:S(2)}, u32[]{:S(2)}) collective-permute-start(bf16[1,1,64,16,256]{4,3,2,1,0:T(8,128)(2,1)S(1)} %bitcast.54), channel_id=1, source_target_pairs={{0,1},{1,2},{2,3},{3,0},{4,5},{5,6},{6,7},{7,4},{8,9},{9,10},{10,1... | collective-permute-start | bytes 1572872 | tf_op jit(solution)/shard_map/ppermute | solution.py:16
  61.6 8.4 %copy-start.6 = (s32[16,8]{0,1:T(8,128)S(1)}, s32[16,8]{0,1:T(8,128)}, u32[]{:S(2)}) copy-start(s32[16,8]{0,1:T(8,128)} %param.26) | copy-start | bytes 1540
  67.3 20.9 %collective-permute-start.5 = (bf16[3,1,64,16,256]{4,3,2,1,0:T(8,128)(2,1)}, bf16[3,1,64,16,256]{4,3,2,1,0:T(8,128)(2,1)}, u32[]{:S(2)}, u32[]{:S(2)}) collective-permute-start(bf16[3,1,64,16,256]{4,3,2,1,0:T(8,128)(2,1)} %pad_maximum_fusion.1), channel_id=1, source_target_pairs={{4,0},{8,4},{12,8},{16,12},{20,16},{24,20},{28,24},{32,28},{36,32}... | collective-permute-start | bytes 4718600 | tf_op jit(solution)/shard_map/ppermute | solution.py:18
  69.9 23.5 %collective-permute-start.4 = (bf16[3,1,64,16,256]{4,3,2,1,0:T(8,128)(2,1)}, bf16[3,1,64,16,256]{4,3,2,1,0:T(8,128)(2,1)}, u32[]{:S(2)}, u32[]{:S(2)}) collective-permute-start(bf16[3,1,64,16,256]{4,3,2,1,0:T(8,128)(2,1)} %pad_maximum_fusion.1), channel_id=1, source_target_pairs={{0,4},{4,8},{8,12},{12,16},{16,20},{20,24},{24,28},{28,32},{32,36}... | collective-permute-start | bytes 4718600 | tf_op jit(solution)/shard_map/ppermute | solution.py:16
  73.3 5.0 %copy-start.4 = (f32[16,16,64]{2,0,1:T(8,128)S(1)}, f32[16,16,64]{2,0,1:T(8,128)}, u32[]{:S(2)}) copy-start(f32[16,16,64]{2,0,1:T(8,128)} %fusion.43) | copy-start | bytes 196612
  73.3 5.4 %copy-start.3 = (f32[64,64,64]{2,1,0:T(8,128)S(1)}, f32[64,64,64]{2,1,0:T(8,128)}, u32[]{:S(2)}) copy-start(f32[64,64,64]{2,1,0:T(8,128)} %param.18) | copy-start | bytes 3145732
where the time goes:
time: 110 us; the launch traced here: 109 us
  blocking collectives  41.1 us (37%)
  matrix products  23.8 us (22%)
  starting transfers between devices  11.5 us (10%)
  other arithmetic  11.3 us (10%)
  waiting for transfers between devices  11.1 us (10%)
  local copies, waits for them, and re-layouts  10.3 us (9%)
    all_gather x1, blocking collectives, shards(): lax.all_gather(partial_top[None], ('slab', 'leaf'), axis=0, tiled=True)  41.1 us
    ppermute x3, starting transfers between devices, padded_2(): lax.ppermute(head, axis, [((i + 1) % count, i) for i in range(count)])  11.5 us
    concatenate x3, other arithmetic, padded_2(): jnp.concatenate([lax.ppermute(tail, axis, [(i, (i + 1) % count) for i in...  7.21 us
    gather x1, local copies, waits for them, and re-layouts, shards(): gathered = flat_sources[near_slot]  6.87 us
    ppermute x3, waiting for transfers between devices, padded_2(): lax.ppermute(head, axis, [((i + 1) % count, i) for i in range(count)])  5.88 us
    ppermute x3, waiting for transfers between devices, padded_2(): lax.ppermute(tail, axis, [(i, (i + 1) % count) for i in range(count)])  5.23 us
    dot_general x1, matrix products, shards(): jnp.einsum('bjrp,jpq->brq', gathered, near_blocks, preferred_element_type...  5.14 us
    dot_general x1, matrix products, shards(): jnp.einsum('qjrk,qjkl->qrl', coupled, section_coupling, precision=highest)  4.94 us
  transfers between devices with their start and end apart: 6, of which 2 were waited for; matrix products, arithmetic and copies ran while one was open for 22% of the time, Pallas kernels for 0%

commit v1 on v0

v1 whole, which is shorter than its diff:
```python
import jax
import jax.numpy as jnp
from jax import lax
from jax.experimental import pallas as pl
from jax.experimental.pallas import tpu as pltpu
from jax.sharding import PartitionSpec as P

GROUP = 4
F32 = jnp.float32
BF16 = jnp.bfloat16
VMEM_LIMIT = 64 * 1024 * 1024
ANY = pl.BlockSpec(memory_space=pl.ANY)
SMEM = pl.BlockSpec(memory_space=pltpu.SMEM)


def dot(a, b):
    return jnp.dot(a, b, preferred_element_type=F32)


def split(x):
    hi = x.astype(BF16)
    return hi, (x - hi.astype(F32)).astype(BF16)


def dot_split(x, w):
    rows = x.shape[0]
    hi, lo = split(x)
    w_hi, w_lo = split(w)
    both = dot(jnp.concatenate([hi, lo], axis=0), w_hi)
    return both[:rows] + both[rows:] + dot(hi, w_lo)


def own_mask(rhs, rank):
    row = lax.broadcasted_iota(jnp.int32, (4 * rhs, 4 * rank), 0) // rhs
    col = lax.broadcasted_iota(jnp.int32, (4 * rhs, 4 * rank), 1) // rank
    return row == col


def moments_kernel(
    parent, sources, source_basis, up_leaf, up_section, pack, top,
    src, basis, lift, raise_, total, out, sems, out_sems,
):
    count, rhs, points = src.shape
    rank = basis.shape[1]
    sections = total.shape[0]
    chunks = 4
    boxes = count // chunks
    keep = pltpu.make_async_copy(src, pack.at[pl.ds(0, count)], out_sems.at[0])
    copies = []
    for c in range(chunks):
        at = pl.ds(c * boxes, boxes)
        copies.append(
            [
                pltpu.make_async_copy(ref.at[at], buf.at[at], sems.at[3 * c + k])
                for k, (ref, buf) in enumerate(((sources, src), (source_basis, basis), (up_leaf, lift)))
            ]
        )
    last = pltpu.make_async_copy(up_section, raise_, sems.at[3 * chunks])
    for group in copies:
        for copy in group:
            copy.start()
    last.start()
    total[...] = jnp.zeros_like(total)
    own = own_mask(rhs, rank)
    for c in range(chunks):
        for copy in copies[c]:
            copy.wait()
        parts = [slice(c * boxes + 4 * f, c * boxes + 4 * f + 4) for f in range(boxes // 4)]
        crossed = [
            lax.dot_general(
                src[part].reshape(4 * rhs, points),
                basis[part].reshape(4 * rank, points),
                (((1,), (1,)), ((), ())),
                preferred_element_type=F32,
            )
            for part in parts
        ]
        lifted = [
            dot_split(jnp.where(own, x, 0.0), lift[part].reshape(4 * rank, rank))
            for x, part in zip(crossed, parts)
        ]
        for f, x in enumerate(lifted):
            for one in range(4):
                slot = parent[c * boxes + 4 * f + one] % sections
                total[slot] += x[one * rhs : (one + 1) * rhs]
    keep.start()
    last.wait()
    for four in range(sections // 4):
        wide = jnp.concatenate([total[4 * four + one] for one in range(4)], axis=1)
        out[four] = wide.astype(BF16)
        term = dot_split(wide, raise_[4 * four : 4 * four + 4].reshape(4 * rank, rank))
        partial = term if four == 0 else partial + term
    half = rhs // 2
    packed = jnp.concatenate([partial[:half], partial[half:]], axis=1).astype(BF16)
    top[...] = jnp.broadcast_to(packed[None], top.shape)
    tail = pltpu.make_async_copy(out, pack.at[pl.ds(count, sections // 4)], out_sems.at[1])
    tail.start()
    tail.wait()
    keep.wait()


def moments_call(parent, sources, source_basis, up_leaf, up_section, devices):
    count, rhs, points = sources.shape
    rank = source_basis.shape[1]
    sections = up_section.shape[0]
    return pl.pallas_call(
        moments_kernel,
        in_specs=[SMEM, ANY, ANY, ANY, ANY],
        out_specs=[ANY, pl.BlockSpec(memory_space=pltpu.VMEM)],
        out_shape=[
            jax.ShapeDtypeStruct((count + sections // 4, rhs, points), BF16),
            jax.ShapeDtypeStruct((devices, rhs // 2, 2 * rank), BF16),
        ],
        scratch_shapes=[
            pltpu.VMEM(sources.shape, BF16),
            pltpu.VMEM(source_basis.shape, BF16),
            pltpu.VMEM(up_leaf.shape, F32),
            pltpu.VMEM(up_section.shape, F32),
            pltpu.VMEM((sections, rhs, rank), F32),
            pltpu.VMEM((sections // 4, rhs, 4 * rank), BF16),
            pltpu.SemaphoreType.DMA((13,)),
            pltpu.SemaphoreType.DMA((2,)),
        ],
        compiler_params=pltpu.CompilerParams(vmem_limit_bytes=VMEM_LIMIT),
        cost_estimate=pl.CostEstimate(flops=0, bytes_accessed=0, transcendentals=0),
        name="moments",
    )(parent, sources, source_basis, up_leaf, up_section)


def coupled_kernel(
    slots, low, high, coupling, out,
    beside, weights, left, right, sems,
):
    sections, rhs, rank = out.shape
    links = coupling.shape[1]
    fours = sections // 4
    count = low.shape[0] - fours
    near = [
        pltpu.make_async_copy(ref.at[pl.ds(count, fours)], beside.at[k], sems.at[k])
        for k, ref in enumerate((low, high))
    ]
    chunks = 4
    here = sections // chunks
    loads = [
        pltpu.make_async_copy(
            coupling.at[pl.ds(c * here, here)], weights.at[pl.ds(c * here, here)], sems.at[2 + c]
        )
        for c in range(chunks)
    ]
    for copy in near + loads:
        copy.start()
    for copy in near:
        copy.wait()
    zero = jnp.zeros((rhs, rank), F32)
    for side in range(2):
        for four in range(fours):
            wide = beside[side, four].astype(F32)
            for one in range(4):
                value = wide[:, one * rank : (one + 1) * rank]
                at = side * sections + 4 * four + one
                left[at] = jnp.concatenate([value, zero], axis=1).astype(BF16)
                right[at] = jnp.concatenate([zero, value], axis=1).astype(BF16)
    for c in range(chunks):
        loads[c].wait()
        for q in range(c * here, (c + 1) * here):
            pairs = [
                left[slots[q * links + j]] + right[slots[q * links + j + 1]]
                for j in range(0, links, 2)
            ]
            wide = jnp.concatenate(pairs, axis=1)
            out[q] = dot(wide, weights[q].reshape(links * rank, rank).astype(BF16))


def coupled_call(slots, low, high, coupling):
    sections, links, rank = coupling.shape[:3]
    rhs, points = low.shape[1:]
    vmem = pl.BlockSpec(memory_space=pltpu.VMEM)
    return pl.pallas_call(
        coupled_kernel,
        in_specs=[SMEM, ANY, ANY, ANY],
        out_specs=vmem,
        out_shape=jax.ShapeDtypeStruct((sections, rhs, rank), F32),
        scratch_shapes=[
            pltpu.VMEM((2, sections // 4, rhs, points), BF16),
            pltpu.VMEM(coupling.shape, F32),
            pltpu.VMEM((2 * sections, rhs, 2 * rank), BF16),
            pltpu.VMEM((2 * sections, rhs, 2 * rank), BF16),
            pltpu.SemaphoreType.DMA((6,)),
        ],
        compiler_params=pltpu.CompilerParams(vmem_limit_bytes=VMEM_LIMIT),
        cost_estimate=pl.CostEstimate(flops=0, bytes_accessed=0, transcendentals=0),
        name="coupled",
    )(slots, low, high, coupling)


def far_kernel(
    parent, links, tops, couplers, down_section, coupled, down_leaf, target, out,
    tops_v, coupler, section_w, coupled_v, leaf_w, target_w, tables, spread, sems,
):
    count, rank, points = target.shape
    sections, rhs, _ = coupled.shape
    link_count = coupler.shape[0]
    slabs = 4
    pairs = (
        (tops, tops_v), (couplers.at[links[0]], coupler), (down_section, section_w),
        (coupled, coupled_v), (down_leaf, leaf_w), (target, target_w),
    )
    loads = [pltpu.make_async_copy(ref, buf, sems.at[k]) for k, (ref, buf) in enumerate(pairs)]
    for copy in loads:
        copy.start()

    for copy in loads[:4]:
        copy.wait()
    half = rhs // 2
    lane = lax.broadcasted_iota(jnp.int32, (half, 2 * rank), 1) < rank
    sums = []
    for j in range(link_count):
        link = links[1 + j]
        first = (link % 8) * (4 * slabs) + link // 8
        total = tops_v[first].astype(F32)
        for one in range(1, 4):
            total += tops_v[first + one * slabs].astype(F32)
        sums.append(total)
    wide = []
    for j in range(0, link_count, 2):
        upper = jnp.where(lane, sums[j], pltpu.roll(sums[j + 1], rank, 1))
        lower = jnp.where(lane, pltpu.roll(sums[j], rank, 1), sums[j + 1])
        wide.append(jnp.concatenate([upper, lower], axis=0))
    local = dot_split(jnp.concatenate(wide, axis=1), coupler[...].reshape(link_count * rank, rank))
    zero = jnp.zeros((rhs, rank), F32)
    for q in range(sections):
        value = dot_split(local, section_w[q]) + coupled_v[q]
        tables[0, q], tables[1, q] = split(jnp.concatenate([value, zero], axis=1))
        tables[2, q], tables[3, q] = split(jnp.concatenate([zero, value], axis=1))

    loads[4].wait()
    mask = own_mask(rhs, rank)
    none = jnp.zeros((rhs, 2 * rank), BF16)
    for four in range(count // 4):
        slot = [parent[4 * four + one] % sections for one in range(4)]
        rows = []
        for part in range(2):
            a, b = tables.at[part], tables.at[2 + part]
            rows += [
                jnp.concatenate([a[slot[0]], none], axis=1),
                jnp.concatenate([b[slot[1]], none], axis=1),
                jnp.concatenate([none, a[slot[2]]], axis=1),
                jnp.concatenate([none, b[slot[3]]], axis=1),
            ]
        w_hi, w_lo = split(leaf_w[4 * four : 4 * four + 4].reshape(4 * rank, rank))
        both = dot(jnp.concatenate(rows, axis=0), w_hi)
        value = both[: 4 * rhs] + both[4 * rhs :] + dot(jnp.concatenate(rows[:4], axis=0), w_lo)
        double = jnp.concatenate([value, value], axis=1)
        spread[four] = jnp.where(mask, jnp.concatenate([double, double], axis=1), 0.0).astype(BF16)
    loads[5].wait()
    for four in range(count // 4):
        at = pl.ds(4 * four * rhs, 4 * rhs)
        out[at] = dot(spread[four], target_w[4 * four : 4 * four + 4].reshape(4 * rank, points))


def far_call(parent, links, tops, couplers, down_section, coupled, down_leaf, target):
    count, rank, points = target.shape
    sections, rhs, _ = coupled.shape
    return pl.pallas_call(
        far_kernel,
        in_specs=[SMEM] * 2 + [ANY] * 6,
        out_specs=pl.BlockSpec(memory_space=pltpu.VMEM),
        out_shape=jax.ShapeDtypeStruct((count * rhs, points), F32),
        scratch_shapes=[
            pltpu.VMEM(tops.shape, BF16),
            pltpu.VMEM(couplers.shape[1:], F32),
            pltpu.VMEM(down_section.shape, F32),
            pltpu.VMEM(coupled.shape, F32),
            pltpu.VMEM(down_leaf.shape, F32),
            pltpu.VMEM(target.shape, BF16),
            pltpu.VMEM((4, sections, rhs, 2 * rank), BF16),
            pltpu.VMEM((count // 4, 4 * rhs, 4 * rank), BF16),
            pltpu.SemaphoreType.DMA((6,)),
        ],
        compiler_params=pltpu.CompilerParams(vmem_limit_bytes=VMEM_LIMIT),
        cost_estimate=pl.CostEstimate(flops=50_000_000_000, bytes_accessed=6_000_000, transcendentals=0),
        name="far",
    )(parent, links, tops, couplers, down_section, coupled, down_leaf, target)


def near_kernel(
    codes, own_src, left_src, right_src, low_src, high_src, corner_left, corner_right,
    near_blocks, far, out, blocks, wide, near_w, far_v, sems,
):
    count, rhs, points = own_src.shape
    entries = near_blocks.shape[0]
    leaf_rows = pl.ds(0, count)
    places = (
        corner_left.at[0], low_src, corner_right.at[0],
        left_src.at[leaf_rows], own_src, right_src.at[leaf_rows],
        corner_left.at[1], high_src, corner_right.at[1],
    )
    loads = [pltpu.make_async_copy(ref, blocks.at[k], sems.at[k]) for k, ref in enumerate(places)]
    loads.append(pltpu.make_async_copy(near_blocks, near_w, sems.at[9]))
    loads.append(pltpu.make_async_copy(far, far_v, sems.at[10]))
    for copy in loads:
        copy.start()

    for k in range(9):
        loads[k].wait()
        for b in range(count):
            code = codes[k * count + b]
            wide[code // count, pl.ds(b * rhs, rhs)] = blocks[k, code % count]
    loads[9].wait()
    loads[10].wait()
    chunk = 16
    for part in range(count // chunk):
        at = pl.ds(part * chunk * rhs, chunk * rhs)
        total = far_v[at]
        for j in range(entries):
            total += dot(wide[j, at], near_w[j])
        out[pl.ds(part * chunk, chunk)] = total.astype(BF16).reshape(chunk, rhs, points)


def near_call(codes, blocks, near_blocks, far):
    count, rhs, points = blocks[0].shape
    entries = near_blocks.shape[0]
    return pl.pallas_call(
        near_kernel,
        in_specs=[SMEM] + [ANY] * 9,
        out_specs=pl.BlockSpec(memory_space=pltpu.VMEM),
        out_shape=jax.ShapeDtypeStruct((count, rhs, points), BF16),
        scratch_shapes=[
            pltpu.VMEM((9, count, rhs, points), BF16),
            pltpu.VMEM((entries, count * rhs, points), BF16),
            pltpu.VMEM(near_blocks.shape, BF16),
            pltpu.VMEM(far.shape, F32),
            pltpu.SemaphoreType.DMA((11,)),
        ],
        compiler_params=pltpu.CompilerParams(vmem_limit_bytes=VMEM_LIMIT),
        cost_estimate=pl.CostEstimate(flops=1_200_000_000, bytes_accessed=8_000_000, transcendentals=0),
        name="near",
    )(codes, *blocks, near_blocks, far)


def shifted(x, axis, step):
    count = lax.axis_size(axis)
    return lax.ppermute(x, axis, [(i, (i + step) % count) for i in range(count)])


def shards(
    sources, source_basis, target_basis, up_leaf, down_leaf, up_section, down_section,
    section_coupling, top_coupling, near_blocks, leaf_parent, near_list, section_list, top_list,
):
    leaf_count = sources.shape[0]
    section_count = up_section.shape[0]
    leaves = lax.axis_size("leaf")
    slabs = lax.axis_size("slab")
    my_leaf = lax.axis_index("leaf")
    my_slab = lax.axis_index("slab")

    owner = near_list // leaf_count
    rel_slab = (owner // leaves - my_slab + 1) % slabs
    rel_leaf = (owner % leaves - my_leaf + 1) % leaves
    entry = jnp.arange(near_list.shape[1], dtype=jnp.int32)
    code = entry * leaf_count + near_list % leaf_count
    place = rel_slab * 3 + rel_leaf
    found = place[None] == jnp.arange(9, dtype=jnp.int32)[:, None, None]
    codes = jnp.sum(jnp.where(found, code[None], 0), axis=2).reshape(-1)
    side = (section_list // section_count % leaves - my_leaf + 1) % leaves // 2
    side_slot = (side * section_count + section_list % section_count).reshape(-1)
    my_top = my_leaf // GROUP
    links = lax.dynamic_index_in_dim(top_list, my_top, 0, keepdims=False)
    links = jnp.concatenate([my_top[None].astype(jnp.int32), links])

    from_low = shifted(sources, "slab", 1)
    from_high = shifted(sources, "slab", -1)
    pack, sent = moments_call(
        leaf_parent, sources, source_basis, up_leaf, up_section, leaves * slabs
    )
    tops = lax.all_to_all(sent, ("leaf", "slab"), 0, 0, tiled=True)
    left = shifted(pack, "leaf", 1)
    right = shifted(pack, "leaf", -1)
    coupled = coupled_call(side_slot, left, right, section_coupling)
    corners = jnp.stack([from_low, from_high])
    corner_left = shifted(corners, "leaf", 1)
    corner_right = shifted(corners, "leaf", -1)
    far = far_call(
        leaf_parent, links, tops, top_coupling, down_section, coupled, down_leaf, target_basis
    )
    blocks = (sources, left, right, from_low, from_high, corner_left, corner_right)
    return near_call(codes, blocks, near_blocks, far)


def solution(mesh):
    in_specs = (
        P(("slab", "leaf"), None, None),
        P(("slab", "leaf"), None, None),
        P(("slab", "leaf"), None, None),
        P(("slab", "leaf"), None, None),
        P(("slab", "leaf"), None, None),
        P(("slab", "leaf"), None, None),
        P(("slab", "leaf"), None, None),
        P(("slab", "leaf"), None, None, None),
        P("slab", None, None, None),
        P(),
        P(("slab", "leaf")),
        P(("slab", "leaf"), None),
        P(("slab", "leaf"), None),
        P("slab", None),
    )
    out_specs = P(("slab", "leaf"), None, None)
    return jax.shard_map(shards, mesh=mesh, in_specs=in_specs, out_specs=out_specs, check_vma=False)
```

time: 110 us -> 52.8 us (0.48)
  blocking collectives: 41.1 us -> 0 us
  matrix products: 23.8 us -> 0 us
  Pallas kernels: 0 us -> 21.5 us
  starting transfers between devices: 11.5 us -> 20.6 us
  other arithmetic: 11.3 us -> 3.23 us
  local copies, waits for them, and re-layouts: 10.3 us -> 2.89 us
  waiting for transfers between devices: 11.1 us -> 4.19 us
    all_gather x1 -> x0, blocking collectives: 41.1 us -> none  [shards(): lax.all_gather(partial_top[None], ('slab', 'leaf'), axis=0, tiled=True)]
    dot_general x11 -> x0, matrix products: 23.8 us -> none  [the longest x1 5.14 us: shards(): jnp.einsum('bjrp,jpq->brq', gathered, near_blocks, preferred_element_type...]
    pallas_call x0 -> x4, Pallas kernels: none -> 21.5 us  [the longest x1 7.62 us: near_call(): pl.pallas_call(near_kernel, in_specs=[SMEM] + [ANY] * 9, out_specs=pl.Blo...]
    gather x3 -> x0, local copies, waits for them, and re-layouts: 9.79 us -> none  [the longest x1 6.87 us: shards(): gathered = flat_sources[near_slot]]
    ppermute x6, waiting for transfers between devices: 11.1 us -> 4.19 us  [shifted(): lax.ppermute(x, axis, [(i, (i + step) % count) for i in range(count)])]
    concatenate x3 -> x1, other arithmetic: 7.21 us -> 0.61 us  [shards(): links = jnp.concatenate([my_top[None].astype(jnp.int32), links])]
    all_to_all x0 -> x1, starting transfers between devices: none -> 6.13 us  [shards(): tops = lax.all_to_all(sent, ('leaf', 'slab'), 0, 0, tiled=True)]
    ppermute x6, starting transfers between devices: 11.5 us -> 14.5 us  [shifted(): lax.ppermute(x, axis, [(i, (i + step) % count) for i in range(count)])]
  transfers between devices with their start and end apart: 6 -> 7, of which waited for: 2 -> 1; matrix products, arithmetic and copies ran while one was open for 22% -> 10% of each run, Pallas kernels for 0% -> 16%
where the time goes in v1:
time: 52.8 us; the launch traced here: 52.5 us
  Pallas kernels  21.5 us (41%)
  starting transfers between devices  20.6 us (39%)
  waiting for transfers between devices  4.19 us (8%)
  other arithmetic  3.23 us (6%)
  local copies, waits for them, and re-layouts  2.89 us (5%)
    ppermute x6, starting transfers between devices, shifted(): lax.ppermute(x, axis, [(i, (i + step) % count) for i in range(count)])  14.5 us
    pallas_call x1, Pallas kernels, near_call(): pl.pallas_call(near_kernel, in_specs=[SMEM] + [ANY] * 9, out_specs=pl.Blo...  7.62 us
    all_to_all x1, starting transfers between devices, shards(): tops = lax.all_to_all(sent, ('leaf', 'slab'), 0, 0, tiled=True)  6.13 us
    pallas_call x1, Pallas kernels, moments_call(): pl.pallas_call(moments_kernel, in_specs=[SMEM, ANY, ANY, ANY, ANY], out_s...  5.27 us
    pallas_call x1, Pallas kernels, far_call(): pl.pallas_call(far_kernel, in_specs=[SMEM] * 2 + [ANY] * 6, out_specs=pl....  4.82 us
    ppermute x6, waiting for transfers between devices, shifted(): lax.ppermute(x, axis, [(i, (i + step) % count) for i in range(count)])  4.19 us
    pallas_call x1, Pallas kernels, coupled_call(): pl.pallas_call(coupled_kernel, in_specs=[SMEM, ANY, ANY, ANY], out_specs=...  3.77 us
    another operation x1, other arithmetic, shards(): corners = jnp.stack([from_low, from_high])  1.09 us
  transfers between devices with their start and end apart: 7, of which 1 were waited for; matrix products, arithmetic and copies ran while one was open for 10% of the time, Pallas kernels for 16%

profile of v1, /device:TPU:0, one launch (start us, length us, event | category | flops | bytes accessed | tf_op | source)
XLA Modules:
  0.0 52.5 jit_solution(11456202951933076577)
XLA Ops:
  0.0 5.3 %moments.1 = (bf16[68,16,256]{2,1,0:T(8,128)(2,1)}, bf16[128,8,128]{2,1,0:T(8,128)(2,1)}) custom-call(s32[64]{0:T(128)} %parent.3, bf16[64,16,256]{2,1,0:T(8,128)(2,1)} %own_src.1, bf16[64,64,256]{2,1,0:T(8,128)(2,1)} %source_basis.1, f32[64,64,64]{2,1,0:T(8,128)} %up_leaf.1, f32[16,64,64]{2,1,0:T(8,128)} %up_section.1), custom_call_target="tpu_custom_call" | custom-call | tf_op jit(solution)/shard_map/moments/pallas_call | solution.py:106
  5.3 0.1 collective-permute-start
  5.4 6.1 %collective-permute-start.1 = (bf16[68,16,256]{2,1,0:T(8,128)(2,1)}, bf16[68,16,256]{2,1,0:T(8,128)(2,1)}, u32[]{:S(2)}, u32[]{:S(2)}) collective-permute-start(bf16[68,16,256]{2,1,0:T(8,128)(2,1)} %get-tuple-element.7), channel_id=1, source_target_pairs={{0,124},{4,0},{8,4},{12,8},{16,12},{20,16},{24,20},{28,24},{32,28}... | collective-permute-start | bytes 1671176 | tf_op jit(solution)/shard_map/ppermute | solution.py:343
  11.4 1.5 %collective-permute-start.2 = (bf16[64,16,256]{2,1,0:T(8,128)(2,1)}, bf16[64,16,256]{2,1,0:T(8,128)(2,1)S(1)}, u32[]{:S(2)}, u32[]{:S(2)}) collective-permute-start(bf16[64,16,256]{2,1,0:T(8,128)(2,1)} %own_src.1), channel_id=1, source_target_pairs={{0,1},{1,2},{2,3},{3,0},{4,5},{5,6},{6,7},{7,4},{8,9},{9,10},{10,1... | collective-permute-start | bytes 1572872 | tf_op jit(solution)/shard_map/ppermute | solution.py:343
  12.9 1.7 %collective-permute-start.3 = (bf16[64,16,256]{2,1,0:T(8,128)(2,1)}, bf16[64,16,256]{2,1,0:T(8,128)(2,1)S(1)}, u32[]{:S(2)}, u32[]{:S(2)}) collective-permute-start(bf16[64,16,256]{2,1,0:T(8,128)(2,1)} %own_src.1), channel_id=1, source_target_pairs={{0,3},{1,0},{2,1},{3,2},{4,7},{5,4},{6,5},{7,6},{8,11},{9,8},{10,9... | collective-permute-start | bytes 1572872 | tf_op jit(solution)/shard_map/ppermute | solution.py:343
  14.7 6.1 %all-to-all-start = ((bf16[128,8,128]{2,1,0:T(8,128)(2,1)}), bf16[128,8,128]{2,1,0:T(8,128)(2,1)}, u32[]{:S(2)}, u32[]{:S(2)}) async-start(bf16[128,8,128]{2,1,0:T(8,128)(2,1)} %get-tuple-element.8), calls=%async_computation | async-start | bytes 524288 | tf_op jit(solution)/shard_map/all_to_all | solution.py:376
  20.8 0.8 %fusion.4 = (s32[64,9]{0,1:T(8,128)S(1)}, s32[64,9]{0,1:T(8,128)S(1)}) fusion(s32[64,9]{0,1:T(8,128)} %param.25, s32[]{:T(128)S(6)} %axis_index.25, s32[]{:T(128)S(6)} %axis_index.22, s32[9]{0:T(128)S(1)} %iota_multiply_fusion), kind=kLoop, calls=%fused_computation.23 | loop fusion | flops 38592 | bytes 6956 | tf_op jit(solution)/shard_map/add | solution.py:362
  21.7 0.7 %fusion.18 = s32[16,8]{0,1:T(8,128)S(1)} fusion(s32[16,8]{0,1:T(8,128)} %param.26, s32[]{:T(128)S(6)} %axis_index.25), kind=kLoop, calls=%fused_computation.54 | loop fusion | flops 7680 | bytes 1028 | tf_op jit(solution)/shard_map/add | solution.py:366
  22.4 0.7 %dynamic-slice_bitcast_fusion = s32[8]{0:T(128)S(1)} fusion(s32[8,8]{1,0:T(8,128)} %param.27, s32[]{:T(128)S(6)} %select_n.69), kind=kLoop, calls=%fused_computation.60 | loop fusion | bytes 68 | tf_op jit(solution)/shard_map/jit(dynamic_index_in_dim)/squeeze | solution.py:368
  23.1 0.7 %reshape.12.codes = s32[576]{0:T(1024)} reshape(s32[9,64]{1,0:T(8,128)S(1)} %select_reduce_fusion) | data formatting | bytes 4608 | tf_op jit(solution)/shard_map/reshape | solution.py:364
  23.7 0.1 copy.21
  23.8 0.6 %reshape.13.slots = s32[128]{0:T(128)} reshape(s32[16,8]{1,0:T(8,128)S(1)} %copy.21) | data formatting | bytes 1024 | tf_op jit(solution)/shard_map/reshape | solution.py:366
  24.4 0.6 %pad_add_fusion.links = s32[9]{0:T(128)} fusion(s32[8]{0:T(128)S(1)} %dynamic-slice_bitcast_fusion, s32[1]{0:T(128)} %bitcast.2), kind=kLoop, calls=%fused_computation.59 | loop fusion | flops 9 | bytes 72 | tf_op jit(solution)/shard_map/concatenate | solution.py:369
  25.0 0.0 collective-permute-done.2.low_src
  25.1 0.0 copy-start
  25.1 0.0 collective-permute-done.3.high_src
  25.1 0.0 copy-start.1
  25.1 0.8 %copy-done = bf16[64,16,256]{2,1,0:T(8,128)(2,1)} copy-done((bf16[64,16,256]{2,1,0:T(8,128)(2,1)}, bf16[64,16,256]{2,1,0:T(8,128)(2,1)S(1)}, u32[]{:S(2)}) %copy-start) | copy-done | bytes 524312
  25.9 1.1 %pad_maximum_fusion = bf16[2,64,16,256]{3,2,1,0:T(8,128)(2,1)} fusion(bf16[1,64,16,256]{3,2,1,0:T(8,128)(2,1)S(1)} %bitcast.6, bf16[1,64,16,256]{3,2,1,0:T(8,128)(2,1)S(1)} %bitcast.5), kind=kLoop, calls=%fused_computation | loop fusion | flops 524288 | bytes 2097152 | tf_op jit(solution)/shard_map/stack | solution.py:380
  27.0 0.0 copy-done.1
  27.0 0.0 collective-permute-start.4
  27.0 5.1 %collective-permute-start.5 = (bf16[2,64,16,256]{3,2,1,0:T(8,128)(2,1)}, bf16[2,64,16,256]{3,2,1,0:T(8,128)(2,1)}, u32[]{:S(2)}, u32[]{:S(2)}) collective-permute-start(bf16[2,64,16,256]{3,2,1,0:T(8,128)(2,1)} %pad_maximum_fusion), channel_id=1, source_target_pairs={{0,124},{4,0},{8,4},{12,8},{16,12},{20,16},{24,20},{28,24},{32,28}... | collective-permute-start | bytes 3145736 | tf_op jit(solution)/shard_map/ppermute | solution.py:343
  32.0 0.0 collective-permute-done.low.left_src
  32.1 0.0 collective-permute-done.1.high.right_src
  32.1 3.8 %coupled.1 = f32[16,16,64]{2,1,0:T(8,128)} custom-call(s32[128]{0:T(128)} %reshape.13.slots, bf16[68,16,256]{2,1,0:T(8,128)(2,1)} %collective-permute-done.low.left_src, bf16[68,16,256]{2,1,0:T(8,128)(2,1)} %collective-permute-done.1.high.right_src, f32[16,8,64,64]{3,2,1,0:T(8,128)} %coupling.1), custom_call_target="tpu_custom_call" | custom-call | tf_op jit(solution)/shard_map/coupled/pallas_call | solution.py:178
  35.8 0.0 all-to-all-done.tops
  35.8 4.8 %far.1 = f32[1024,256]{1,0:T(8,128)} custom-call(s32[64]{0:T(128)} %parent.3, s32[9]{0:T(128)} %pad_add_fusion.links, bf16[128,8,128]{2,1,0:T(8,128)(2,1)} %all-to-all-done.tops, f32[8,8,64,64]{3,2,1,0:T(8,128)} %couplers.1, f32[16,64,64]{2,1,0:T(8,128)} %down_section.1, f32[16,16,64]{2,1,0:T(8,128)} %coupled.1, f32[64,64,64]{2,1,0:T(8,128)} %down_leaf.1, ...), custom_call_target="tpu_custom_call" | custom-call | flops 49999998976 | bytes 6000000 | tf_op jit(solution)/shard_map/far/pallas_call | solution.py:264
  40.7 4.2 %collective-permute-done.4.corner_left = bf16[2,64,16,256]{3,2,1,0:T(8,128)(2,1)} collective-permute-done((bf16[2,64,16,256]{3,2,1,0:T(8,128)(2,1)}, bf16[2,64,16,256]{3,2,1,0:T(8,128)(2,1)}, u32[]{:S(2)}, u32[]{:S(2)}) %collective-permute-start.4) | collective-permute-done | bytes 1048608 | tf_op jit(solution)/shard_map/ppermute | solution.py:343
  44.8 0.0 collective-permute-done.5.corner_right
  44.8 7.6 %near.1 = bf16[64,16,256]{2,1,0:T(8,128)(2,1)} custom-call(s32[576]{0:T(1024)} %reshape.12.codes, bf16[64,16,256]{2,1,0:T(8,128)(2,1)} %own_src.1, bf16[68,16,256]{2,1,0:T(8,128)(2,1)} %collective-permute-done.low.left_src, bf16[68,16,256]{2,1,0:T(8,128)(2,1)} %collective-permute-done.1.high.right_src, bf16[64,16,256]{2,1,0:T(8,128)(2,1)} %copy-done, ...), custom_call_target="tpu_custom_call" | custom-call | flops 1200000000 | bytes 8000000 | tf_op jit(solution)/shard_map/near/pallas_call | solution.py:323
  (2 shorter events, 0.0 us)
Async XLA Ops:
  5.3 26.8 %collective-permute-start = (bf16[68,16,256]{2,1,0:T(8,128)(2,1)}, bf16[68,16,256]{2,1,0:T(8,128)(2,1)}, u32[]{:S(2)}, u32[]{:S(2)}) collective-permute-start(bf16[68,16,256]{2,1,0:T(8,128)(2,1)} %get-tuple-element.7), channel_id=1, source_target_pairs={{0,4},{4,8},{8,12},{12,16},{16,20},{20,24},{24,28},{28,32},{32,36}... | collective-permute-start | bytes 1671176 | tf_op jit(solution)/shard_map/ppermute | solution.py:343
  5.4 26.7 %collective-permute-start.1 = (bf16[68,16,256]{2,1,0:T(8,128)(2,1)}, bf16[68,16,256]{2,1,0:T(8,128)(2,1)}, u32[]{:S(2)}, u32[]{:S(2)}) collective-permute-start(bf16[68,16,256]{2,1,0:T(8,128)(2,1)} %get-tuple-element.7), channel_id=1, source_target_pairs={{0,124},{4,0},{8,4},{12,8},{16,12},{20,16},{24,20},{28,24},{32,28}... | collective-permute-start | bytes 1671176 | tf_op jit(solution)/shard_map/ppermute | solution.py:343
  11.4 13.6 %collective-permute-start.2 = (bf16[64,16,256]{2,1,0:T(8,128)(2,1)}, bf16[64,16,256]{2,1,0:T(8,128)(2,1)S(1)}, u32[]{:S(2)}, u32[]{:S(2)}) collective-permute-start(bf16[64,16,256]{2,1,0:T(8,128)(2,1)} %own_src.1), channel_id=1, source_target_pairs={{0,1},{1,2},{2,3},{3,0},{4,5},{5,6},{6,7},{7,4},{8,9},{9,10},{10,1... | collective-permute-start | bytes 1572872 | tf_op jit(solution)/shard_map/ppermute | solution.py:343
  12.9 12.1 %collective-permute-start.3 = (bf16[64,16,256]{2,1,0:T(8,128)(2,1)}, bf16[64,16,256]{2,1,0:T(8,128)(2,1)S(1)}, u32[]{:S(2)}, u32[]{:S(2)}) collective-permute-start(bf16[64,16,256]{2,1,0:T(8,128)(2,1)} %own_src.1), channel_id=1, source_target_pairs={{0,3},{1,0},{2,1},{3,2},{4,7},{5,4},{6,5},{7,6},{8,11},{9,8},{10,9... | collective-permute-start | bytes 1572872 | tf_op jit(solution)/shard_map/ppermute | solution.py:343
  14.7 21.2 %all-to-all-start = ((bf16[128,8,128]{2,1,0:T(8,128)(2,1)}), bf16[128,8,128]{2,1,0:T(8,128)(2,1)}, u32[]{:S(2)}, u32[]{:S(2)}) async-start(bf16[128,8,128]{2,1,0:T(8,128)(2,1)} %get-tuple-element.8), calls=%async_computation | async-start | bytes 524288 | tf_op jit(solution)/shard_map/all_to_all | solution.py:376
  25.1 0.8 %copy-start = (bf16[64,16,256]{2,1,0:T(8,128)(2,1)}, bf16[64,16,256]{2,1,0:T(8,128)(2,1)S(1)}, u32[]{:S(2)}) copy-start(bf16[64,16,256]{2,1,0:T(8,128)(2,1)S(1)} %collective-permute-done.2.low_src) | copy-start | bytes 1572868
  25.1 1.9 %copy-start.1 = (bf16[64,16,256]{2,1,0:T(8,128)(2,1)}, bf16[64,16,256]{2,1,0:T(8,128)(2,1)S(1)}, u32[]{:S(2)}) copy-start(bf16[64,16,256]{2,1,0:T(8,128)(2,1)S(1)} %collective-permute-done.3.high_src) | copy-start | bytes 1572868
  27.0 17.9 %collective-permute-start.4 = (bf16[2,64,16,256]{3,2,1,0:T(8,128)(2,1)}, bf16[2,64,16,256]{3,2,1,0:T(8,128)(2,1)}, u32[]{:S(2)}, u32[]{:S(2)}) collective-permute-start(bf16[2,64,16,256]{3,2,1,0:T(8,128)(2,1)} %pad_maximum_fusion), channel_id=1, source_target_pairs={{0,4},{4,8},{8,12},{12,16},{16,20},{20,24},{24,28},{28,32},{32,36}... | collective-permute-start | bytes 3145736 | tf_op jit(solution)/shard_map/ppermute | solution.py:343
  27.0 17.9 %collective-permute-start.5 = (bf16[2,64,16,256]{3,2,1,0:T(8,128)(2,1)}, bf16[2,64,16,256]{3,2,1,0:T(8,128)(2,1)}, u32[]{:S(2)}, u32[]{:S(2)}) collective-permute-start(bf16[2,64,16,256]{3,2,1,0:T(8,128)(2,1)} %pad_maximum_fusion), channel_id=1, source_target_pairs={{0,124},{4,0},{8,4},{12,8},{16,12},{20,16},{24,20},{28,24},{32,28}... | collective-permute-start | bytes 3145736 | tf_op jit(solution)/shard_map/ppermute | solution.py:343

commit v2 on v0

v2 whole, which is shorter than its diff:
```python
import jax
import jax.numpy as jnp
from jax import lax
from jax.experimental import pallas as pl
from jax.experimental.pallas import tpu as pltpu
from jax.sharding import PartitionSpec as P

GROUP = 4
F32 = jnp.float32
BF16 = jnp.bfloat16
HBM = pl.BlockSpec(memory_space=pltpu.HBM)
VMEM = pl.BlockSpec(memory_space=pltpu.VMEM)
SMEM = pl.BlockSpec(memory_space=pltpu.SMEM)
LISTS = 4
PACK = 32


def params(mib=64):
    return pltpu.CompilerParams(vmem_limit_bytes=mib * 1024 * 1024)


def cost(us):
    return pl.CostEstimate(flops=int(us * 1_000_000_000), bytes_accessed=0, transcendentals=0)


def dot(a, b):
    return jnp.dot(a, b, preferred_element_type=F32)


def split(x):
    hi = x.astype(BF16)
    return hi, (x - hi.astype(F32)).astype(BF16)


def dot_split(x, w):
    rows = x.shape[0]
    hi, lo = split(x)
    w_hi, w_lo = split(w)
    both = dot(jnp.concatenate([hi, lo], axis=0), w_hi)
    return both[:rows] + both[rows:] + dot(hi, w_lo)


def own_mask(rhs, rank):
    row = lax.broadcasted_iota(jnp.int32, (4 * rhs, 4 * rank), 0) // rhs
    col = lax.broadcasted_iota(jnp.int32, (4 * rhs, 4 * rank), 1) // rank
    return row == col


def started(pairs, sems):
    copies = [pltpu.make_async_copy(ref, buf, sems.at[k]) for k, (ref, buf) in enumerate(pairs)]
    for copy in copies:
        copy.start()
    return copies


def list_place(entries, count):
    my_leaf = lax.axis_index("leaf")
    my_slab = lax.axis_index("slab")
    leaves = lax.axis_size("leaf")
    slabs = lax.axis_size("slab")
    owner = entries // count
    rel_slab = (owner // leaves - my_slab + 1) & (slabs - 1)
    rel_leaf = ((owner & (leaves - 1)) - my_leaf + 1) & (leaves - 1)
    return rel_leaf, rel_slab * count + (entries & (count - 1))


def moments_kernel(
    parent, sources, source_basis, up_leaf, up_section, near_list, to_inner, to_outer, top,
    src, basis, lift, raise_, lists, total, sems,
):
    count, rhs, points = src.shape
    rank = basis.shape[1]
    sections = total.shape[0]
    chunks = 4
    boxes = count // chunks
    pairs = []
    for c in range(chunks):
        at = pl.ds(c * boxes, boxes)
        pairs += [(ref.at[at], buf.at[at]) for ref, buf in ((sources, src), (source_basis, basis), (up_leaf, lift))]
        if c == 0:
            pairs += [(near_list, lists), (up_section, raise_)]
    copies = started(pairs, sems)
    total[...] = jnp.zeros_like(total)
    to_inner[...] = jnp.zeros_like(to_inner)
    to_outer[...] = jnp.zeros_like(to_outer)
    own = own_mask(rhs, rank)
    at_copy = 0
    for c in range(chunks):
        many = 5 if c == 0 else 3
        for copy in copies[at_copy : at_copy + many]:
            copy.wait()
        at_copy += many
        parts = [slice(c * boxes + 4 * f, c * boxes + 4 * f + 4) for f in range(boxes // 4)]
        crossed = [
            lax.dot_general(
                src[part].reshape(4 * rhs, points),
                basis[part].reshape(4 * rank, points),
                (((1,), (1,)), ((), ())),
                preferred_element_type=F32,
            )
            for part in parts
        ]
        lifted = [
            dot_split(jnp.where(own, x, 0.0), lift[part].reshape(4 * rank, rank))
            for x, part in zip(crossed, parts)
        ]
        for f, x in enumerate(lifted):
            for one in range(4):
                slot = parent[c * boxes + 4 * f + one] & (sections - 1)
                total[slot] += x[one * rhs : (one + 1) * rhs]
    fours = sections // 4
    for four in range(fours):
        wide = jnp.concatenate([total[4 * four + one] for one in range(4)], axis=1)
        to_inner[four] = wide.astype(BF16)
        to_outer[four] = wide.astype(BF16)
        term = dot_split(wide, raise_[4 * four : 4 * four + 4].reshape(4 * rank, rank))
        partial = term if four == 0 else partial + term
    half = rhs // 2
    packed = jnp.concatenate([partial[:half], partial[half:]], axis=1).astype(BF16)
    top[...] = jnp.broadcast_to(packed[None], top.shape)

    entries = lists[...]
    rel_leaf, place = list_place(entries, count)
    rows, boxes = entries.shape
    odd = lax.axis_index("leaf") & 1
    for ref, step in ((to_inner, 2 - 2 * odd), (to_outer, 2 * odd)):
        ref[fours, :rows, :boxes] = jnp.where(rel_leaf == step, place, 3 * count).astype(F32).astype(BF16)


def moments_call(parent, sources, source_basis, up_leaf, up_section, near_list, devices):
    count, rhs, points = sources.shape
    rank = source_basis.shape[1]
    sections = up_section.shape[0]
    pack = jax.ShapeDtypeStruct((PACK, rhs, points), BF16)
    return pl.pallas_call(
        moments_kernel,
        in_specs=[SMEM, HBM, HBM, HBM, HBM, HBM],
        out_specs=[VMEM, VMEM, VMEM],
        out_shape=[pack, pack, jax.ShapeDtypeStruct((devices, rhs // 2, 2 * rank), BF16)],
        scratch_shapes=[
            pltpu.VMEM(sources.shape, BF16),
            pltpu.VMEM(source_basis.shape, BF16),
            pltpu.VMEM(up_leaf.shape, F32),
            pltpu.VMEM(up_section.shape, F32),
            pltpu.VMEM(near_list.shape, jnp.int32),
            pltpu.VMEM((sections, rhs, rank), F32),
            pltpu.SemaphoreType.DMA((14,)),
        ],
        compiler_params=params(),
        cost_estimate=cost(0),
        name="moments",
    )(parent, sources, source_basis, up_leaf, up_section, near_list)


def near_sum(codes, table, near_blocks, store):
    entries = near_blocks.shape[0]
    count = 64
    chunk = 16
    for part in range(count // chunk):
        for j in range(entries):
            rows = jnp.concatenate([table[codes(j, part * chunk + b)] for b in range(chunk)], axis=0)
            term = dot(rows, near_blocks[j])
            total = term if j == 0 else total + term
        store(part * chunk, chunk, total)


def beside_kernel(
    inner, outer, from_low, own_src, from_high, near_list, near_blocks,
    to_inner, to_outer, own_codes, table, near_w, lists, entries, coded, codes, sems, code_sems,
):
    count, rhs, points = own_src.shape
    fours = LISTS
    copies = started(
        (
            (inner.at[fours], lists.at[0]), (outer.at[fours], lists.at[1]), (near_list, entries),
            (near_blocks, near_w),
            (from_low, table.at[pl.ds(0, count)]),
            (own_src, table.at[pl.ds(count, count)]),
            (from_high, table.at[pl.ds(2 * count, count)]),
        ),
        sems,
    )
    table[3 * count] = jnp.zeros((rhs, points), BF16)
    for copy in copies[:3]:
        copy.wait()
    rel_leaf, place = list_place(entries[...], count)
    own_codes[...] = jnp.where(rel_leaf == 1, place, 3 * count)
    for k in range(2):
        coded[k] = lists[k].astype(F32).astype(jnp.int32)[:, :128]
    moves = [pltpu.make_async_copy(coded.at[k], codes.at[k], code_sems.at[k]) for k in range(2)]
    for move in moves:
        move.start()
    for copy in copies[3:]:
        copy.wait()
    for move in moves:
        move.wait()
    for k, out in enumerate((to_inner, to_outer)):
        def store(at, many, total, out=out):
            out[pl.ds(at, many)] = total.astype(BF16).reshape(many, rhs, points)

        near_sum(lambda j, b, k=k: codes[k, j, b], table, near_w, store)


def beside_call(inner, outer, from_low, own_src, from_high, near_list, near_blocks):
    count, rhs, points = own_src.shape
    block = jax.ShapeDtypeStruct(own_src.shape, BF16)
    return pl.pallas_call(
        beside_kernel,
        in_specs=[HBM] * 7,
        out_specs=[VMEM] * 3,
        out_shape=[block, block, jax.ShapeDtypeStruct(near_list.shape, jnp.int32)],
        scratch_shapes=[
            pltpu.VMEM((3 * count + 1, rhs, points), BF16),
            pltpu.VMEM(near_blocks.shape, BF16),
            pltpu.VMEM((2, rhs, points), BF16),
            pltpu.VMEM(near_list.shape, jnp.int32),
            pltpu.VMEM((2, rhs, 128), jnp.int32),
            pltpu.SMEM((2, rhs, 128), jnp.int32),
            pltpu.SemaphoreType.DMA((7,)),
            pltpu.SemaphoreType.DMA((2,)),
        ],
        compiler_params=params(),
        cost_estimate=cost(0),
        name="beside",
    )(inner, outer, from_low, own_src, from_high, near_list, near_blocks)


def local_kernel(
    parent, top_links, links, codes,
    inner, outer, coupling, from_low, own_src, from_high, near_blocks, tops, couplers, down_section,
    down_leaf, target, out,
    table, near_w, beside, couple_w, tops_v, coupler, section_w, leaf_w, target_w,
    left, right, coupled, tables, spread, sems,
):
    count, rhs, points = out.shape
    rank = target.shape[1]
    sections, link_count = coupling.shape[:2]
    fours = sections // 4
    my_leaf = lax.axis_index("leaf")
    leaves = lax.axis_size("leaf")
    slabs = lax.axis_size("slab")
    my_top = my_leaf // GROUP
    chunks = 4
    here = sections // chunks
    pairs = [(inner.at[pl.ds(0, fours)], beside.at[0]), (outer.at[pl.ds(0, fours)], beside.at[1])]
    for c in range(chunks):
        at = pl.ds(c * here, here)
        pairs.append((coupling.at[at], couple_w.at[at]))
    pairs += [
        (near_blocks, near_w),
        (from_low, table.at[pl.ds(0, count)]),
        (own_src, table.at[pl.ds(count, count)]),
        (from_high, table.at[pl.ds(2 * count, count)]),
        (tops, tops_v), (couplers.at[my_top], coupler), (down_section, section_w),
        (down_leaf, leaf_w), (target, target_w),
    ]
    copies = started(pairs, sems)

    table[3 * count] = jnp.zeros((rhs, points), BF16)

    for copy in copies[:2]:
        copy.wait()
    zero = jnp.zeros((rhs, rank), F32)
    for side in range(2):
        for four in range(fours):
            wide = beside[side, four].astype(F32)
            for one in range(4):
                value = wide[:, one * rank : (one + 1) * rank]
                at = side * sections + 4 * four + one
                left[at] = jnp.concatenate([value, zero], axis=1).astype(BF16)
                right[at] = jnp.concatenate([zero, value], axis=1).astype(BF16)

    def slot(j, q):
        entry = links[j, q]
        leaf = (entry // sections) & (leaves - 1)
        return jnp.where(leaf == my_leaf ^ 1, 0, sections) + (entry & (sections - 1))

    for q in range(sections):
        if q % here == 0:
            copies[2 + q // here].wait()
        pairs = [left[slot(j, q)] + right[slot(j + 1, q)] for j in range(0, link_count, 2)]
        wide = jnp.concatenate(pairs, axis=1)
        coupled[q] = dot(wide, couple_w[q].reshape(link_count * rank, rank).astype(BF16))

    for copy in copies[6:10]:
        copy.wait()

    def store(at, many, total):
        out[pl.ds(at, many)] = total.reshape(many, rhs, points)

    near_sum(lambda j, b: codes[j, b], table, near_w, store)

    for copy in copies[10:13]:
        copy.wait()
    slab_tops = top_links.shape[0]
    half = rhs // 2
    lane = lax.broadcasted_iota(jnp.int32, (half, 2 * rank), 1) < rank
    sums = []
    for j in range(link_count):
        link = top_links[my_top, j]
        first = (link & (slab_tops - 1)) * (GROUP * slabs) + link // slab_tops
        sums.append(sum(tops_v[first + one * slabs].astype(F32) for one in range(GROUP)))
    wide = []
    for j in range(0, link_count, 2):
        upper = jnp.where(lane, sums[j], pltpu.roll(sums[j + 1], rank, 1))
        lower = jnp.where(lane, pltpu.roll(sums[j], rank, 1), sums[j + 1])
        wide.append(jnp.concatenate([upper, lower], axis=0))
    local = dot_split(jnp.concatenate(wide, axis=1), coupler[...].reshape(link_count * rank, rank))
    for q in range(sections):
        value = dot_split(local, section_w[q]) + coupled[q]
        tables[0, q], tables[1, q] = split(jnp.concatenate([value, zero], axis=1))
        tables[2, q], tables[3, q] = split(jnp.concatenate([zero, value], axis=1))

    for copy in copies[13:]:
        copy.wait()
    mask = own_mask(rhs, rank)
    none = jnp.zeros((rhs, 2 * rank), BF16)
    for four in range(count // 4):
        slots = [parent[4 * four + one] & (sections - 1) for one in range(4)]
        lines = []
        for part in range(2):
            a, b = tables.at[part], tables.at[2 + part]
            lines += [
                jnp.concatenate([a[slots[0]], none], axis=1),
                jnp.concatenate([b[slots[1]], none], axis=1),
                jnp.concatenate([none, a[slots[2]]], axis=1),
                jnp.concatenate([none, b[slots[3]]], axis=1),
            ]
        w_hi, w_lo = split(leaf_w[4 * four : 4 * four + 4].reshape(4 * rank, rank))
        both = dot(jnp.concatenate(lines, axis=0), w_hi)
        value = both[: 4 * rhs] + both[4 * rhs :] + dot(jnp.concatenate(lines[:4], axis=0), w_lo)
        double = jnp.concatenate([value, value], axis=1)
        spread[four] = jnp.where(mask, jnp.concatenate([double, double], axis=1), 0.0).astype(BF16)
    for four in range(count // 4):
        at = pl.ds(4 * four, 4)
        far = dot(spread[four], target_w[4 * four : 4 * four + 4].reshape(4 * rank, points))
        out[at] += far.reshape(4, rhs, points)


def local_call(
    parent, top_links, links, codes, inner, outer, coupling, from_low, own_src, from_high, near_blocks,
    tops, couplers, down_section, down_leaf, target,
):
    rhs = own_src.shape[1]
    count, rank, points = target.shape
    sections = coupling.shape[0]
    return pl.pallas_call(
        local_kernel,
        in_specs=[SMEM] * 4 + [HBM] * 12,
        out_specs=VMEM,
        out_shape=jax.ShapeDtypeStruct((count, rhs, points), F32),
        scratch_shapes=[
            pltpu.VMEM((3 * count + 1, rhs, points), BF16),
            pltpu.VMEM(near_blocks.shape, BF16),
            pltpu.VMEM((2, sections // 4, rhs, points), BF16),
            pltpu.VMEM(coupling.shape, F32),
            pltpu.VMEM(tops.shape, BF16),
            pltpu.VMEM(couplers.shape[1:], F32),
            pltpu.VMEM(down_section.shape, F32),
            pltpu.VMEM(down_leaf.shape, F32),
            pltpu.VMEM(target.shape, BF16),
            pltpu.VMEM((2 * sections, rhs, 2 * rank), BF16),
            pltpu.VMEM((2 * sections, rhs, 2 * rank), BF16),
            pltpu.VMEM((sections, rhs, rank), F32),
            pltpu.VMEM((4, sections, rhs, 2 * rank), BF16),
            pltpu.VMEM((count // 4, 4 * rhs, 4 * rank), BF16),
            pltpu.SemaphoreType.DMA((15,)),
        ],
        compiler_params=params(),
        cost_estimate=cost(40),
        name="local",
    )(
        parent, top_links, links, codes, inner, outer, coupling, from_low, own_src, from_high, near_blocks,
        tops, couplers, down_section, down_leaf, target,
    )


def shifted(x, axis, step):
    count = lax.axis_size(axis)
    return lax.ppermute(x, axis, [(i, (i + step) % count) for i in range(count)])


def swapped(x, first):
    count = lax.axis_size("leaf")
    return lax.ppermute(
        x, "leaf", [(i, (i + (1 if i % 2 == first else -1)) % count) for i in range(count)]
    )


def shards(
    sources, source_basis, target_basis, up_leaf, down_leaf, up_section, down_section,
    section_coupling, top_coupling, near_blocks, leaf_parent, near_list, section_list, top_list,
):
    devices = lax.axis_size("leaf") * lax.axis_size("slab")
    near_list = near_list.T
    from_low = shifted(sources, "slab", 1)
    from_high = shifted(sources, "slab", -1)
    to_inner, to_outer, sent = moments_call(
        leaf_parent, sources, source_basis, up_leaf, up_section, near_list, devices
    )
    inner = swapped(to_inner, 0)
    outer = swapped(to_outer, 1)
    tops = lax.all_to_all(sent, ("leaf", "slab"), 0, 0, tiled=True)
    near_inner, near_outer, codes = beside_call(
        inner, outer, from_low, sources, from_high, near_list, near_blocks
    )
    near_inner = swapped(near_inner, 0)
    near_outer = swapped(near_outer, 1)
    local = local_call(
        leaf_parent, top_list, section_list.T, codes, inner, outer, section_coupling, from_low, sources,
        from_high, near_blocks, tops, top_coupling, down_section, down_leaf, target_basis,
    )
    return (local + near_inner.astype(F32) + near_outer.astype(F32)).astype(BF16)


def solution(mesh):
    in_specs = (
        P(("slab", "leaf"), None, None),
        P(("slab", "leaf"), None, None),
        P(("slab", "leaf"), None, None),
        P(("slab", "leaf"), None, None),
        P(("slab", "leaf"), None, None),
        P(("slab", "leaf"), None, None),
        P(("slab", "leaf"), None, None),
        P(("slab", "leaf"), None, None, None),
        P("slab", None, None, None),
        P(),
        P(("slab", "leaf")),
        P(("slab", "leaf"), None),
        P(("slab", "leaf"), None),
        P("slab", None),
    )
    out_specs = P(("slab", "leaf"), None, None)
    return jax.shard_map(shards, mesh=mesh, in_specs=in_specs, out_specs=out_specs, check_vma=False)
```

time: 110 us -> 43 us (0.39)
  the two profiles are of different devices: /device:TPU:0 before, /device:TPU:1 now
where the time goes in v2:
time: 43 us; the launch traced here: 42.8 us
  starting transfers between devices  18.3 us (43%)
  Pallas kernels  18.2 us (42%)
  waiting for transfers between devices  3.68 us (9%)
  other arithmetic  2.53 us (6%)
    all_to_all x1, starting transfers between devices, shards(): tops = lax.all_to_all(sent, ('leaf', 'slab'), 0, 0, tiled=True)  10.3 us
    pallas_call x1, Pallas kernels, local_call(): pl.pallas_call(local_kernel, in_specs=[SMEM] * 4 + [HBM] * 12, out_specs=...  7.75 us
    pallas_call x1, Pallas kernels, beside_call(): pl.pallas_call(beside_kernel, in_specs=[HBM] * 7, out_specs=[VMEM] * 3, o...  5.27 us
    pallas_call x1, Pallas kernels, moments_call(): pl.pallas_call(moments_kernel, in_specs=[SMEM, HBM, HBM, HBM, HBM, HBM],...  5.18 us
    ppermute x4, starting transfers between devices, swapped(): lax.ppermute(x, 'leaf', [(i, (i + (1 if i % 2 == first else -1)) % count)...  4.63 us
    all_to_all x1, waiting for transfers between devices, shards(): tops = lax.all_to_all(sent, ('leaf', 'slab'), 0, 0, tiled=True)  3.67 us
    ppermute x2, starting transfers between devices, shifted(): lax.ppermute(x, axis, [(i, (i + step) % count) for i in range(count)])  3.31 us
    convert_element_type x1, other arithmetic, shards(): (local + near_inner.astype(F32) + near_outer.astype(F32)).astype(BF16)  2.53 us
  transfers between devices with their start and end apart: 7, of which 1 were waited for; matrix products, arithmetic and copies ran while one was open for 0% of the time, Pallas kernels for 43%

profile of v2, /device:TPU:1, one launch (start us, length us, event | category | flops | bytes accessed | tf_op | source)
XLA Modules:
  0.0 42.8 jit_solution(10765399755018797397)
XLA Ops:
  0.0 3.3 %collective-permute-start.3 = (bf16[64,16,256]{2,1,0:T(8,128)(2,1)}, bf16[64,16,256]{2,1,0:T(8,128)(2,1)}, u32[]{:S(2)}, u32[]{:S(2)}) collective-permute-start(bf16[64,16,256]{2,1,0:T(8,128)(2,1)} %own_src.3), channel_id=1, source_target_pairs={{0,3},{1,0},{2,1},{3,2},{4,7},{5,4},{6,5},{7,6},{8,11},{9,8},{10,9... | collective-permute-start | bytes 1572872 | tf_op jit(solution)/shard_map/ppermute | solution.py:380
  3.3 0.0 collective-permute-start.2
  3.3 5.2 %moments.1 = (bf16[32,16,256]{2,1,0:T(8,128)(2,1)}, bf16[32,16,256]{2,1,0:T(8,128)(2,1)}, bf16[128,8,128]{2,1,0:T(8,128)(2,1)}) custom-call(s32[64]{0:T(128)} %parent.3, bf16[64,16,256]{2,1,0:T(8,128)(2,1)} %own_src.3, bf16[64,64,256]{2,1,0:T(8,128)(2,1)} %source_basis.1, f32[64,64,64]{2,1,0:T(8,128)} %up_leaf.1, f32[16,64,64]{2,1,0:T(8,128)} %up_section.1, ...), custom_call_target="tpu_custom_call" | custom-call | tf_op jit(solution)/shard_map/moments/pallas_call | solution.py:135
  8.5 1.0 %collective-permute-start = (bf16[32,16,256]{2,1,0:T(8,128)(2,1)}, bf16[32,16,256]{2,1,0:T(8,128)(2,1)}, u32[]{:S(2)}, u32[]{:S(2)}) collective-permute-start(bf16[32,16,256]{2,1,0:T(8,128)(2,1)} %get-tuple-element.11), channel_id=1, source_target_pairs={{0,4},{4,0},{8,12},{12,8},{16,20},{20,16},{24,28},{28,24},{32,36},... | collective-permute-start | bytes 786440 | tf_op jit(solution)/shard_map/ppermute | solution.py:385
  9.5 1.6 %collective-permute-start.1 = (bf16[32,16,256]{2,1,0:T(8,128)(2,1)}, bf16[32,16,256]{2,1,0:T(8,128)(2,1)}, u32[]{:S(2)}, u32[]{:S(2)}) collective-permute-start(bf16[32,16,256]{2,1,0:T(8,128)(2,1)} %get-tuple-element.12), channel_id=1, source_target_pairs={{0,124},{4,8},{8,4},{12,16},{16,12},{20,24},{24,20},{28,32},{32,28... | collective-permute-start | bytes 786440 | tf_op jit(solution)/shard_map/ppermute | solution.py:385
  11.1 10.3 %all-to-all-start = ((bf16[128,8,128]{2,1,0:T(8,128)(2,1)}), bf16[128,8,128]{2,1,0:T(8,128)(2,1)}, u32[]{:S(2)}, u32[]{:S(2)}) async-start(bf16[128,8,128]{2,1,0:T(8,128)(2,1)} %get-tuple-element.14), calls=%async_computation | async-start | bytes 524288 | tf_op jit(solution)/shard_map/all_to_all | solution.py:403
  21.5 0.0 collective-permute-done.inner
  21.5 0.0 collective-permute-done.1.outer
  21.5 0.0 collective-permute-done.3.from_high
  21.5 0.0 collective-permute-done.2.from_low
  21.5 5.3 %beside.1 = (bf16[64,16,256]{2,1,0:T(8,128)(2,1)}, bf16[64,16,256]{2,1,0:T(8,128)(2,1)}, s32[9,64]{1,0:T(8,128)}) custom-call(bf16[32,16,256]{2,1,0:T(8,128)(2,1)} %collective-permute-done.inner, bf16[32,16,256]{2,1,0:T(8,128)(2,1)} %collective-permute-done.1.outer, bf16[64,16,256]{2,1,0:T(8,128)(2,1)} %collective-permute-done.2.from_low, ...), custom_call_target="tpu_custom_call" | custom-call | tf_op jit(solution)/shard_map/beside/pallas_call | solution.py:207
  26.8 1.2 %collective-permute-start.4 = (bf16[64,16,256]{2,1,0:T(8,128)(2,1)}, bf16[64,16,256]{2,1,0:T(8,128)(2,1)}, u32[]{:S(2)}, u32[]{:S(2)}) collective-permute-start(bf16[64,16,256]{2,1,0:T(8,128)(2,1)} %get-tuple-element.15), channel_id=1, source_target_pairs={{0,4},{4,0},{8,12},{12,8},{16,20},{20,16},{24,28},{28,24},{32,36},... | collective-permute-start | bytes 1572872 | tf_op jit(solution)/shard_map/ppermute | solution.py:385
  28.0 0.8 %collective-permute-start.5 = (bf16[64,16,256]{2,1,0:T(8,128)(2,1)}, bf16[64,16,256]{2,1,0:T(8,128)(2,1)}, u32[]{:S(2)}, u32[]{:S(2)}) collective-permute-start(bf16[64,16,256]{2,1,0:T(8,128)(2,1)} %get-tuple-element.16), channel_id=1, source_target_pairs={{0,124},{4,8},{8,4},{12,16},{16,12},{20,24},{24,20},{28,32},{32,28... | collective-permute-start | bytes 1572872 | tf_op jit(solution)/shard_map/ppermute | solution.py:385
  28.8 3.7 %all-to-all-done.tops = bf16[128,8,128]{2,1,0:T(8,128)(2,1)} async-done(((bf16[128,8,128]{2,1,0:T(8,128)(2,1)}), bf16[128,8,128]{2,1,0:T(8,128)(2,1)}, u32[]{:S(2)}, u32[]{:S(2)}) %all-to-all-start) | async-done | bytes 262176 | tf_op jit(solution)/shard_map/all_to_all | solution.py:403
  32.5 7.7 %local.1 = f32[64,16,256]{2,1,0:T(8,128)} custom-call(s32[64]{0:T(128)} %parent.3, s32[8,8]{1,0:T(8,128)} %top_links.1, s32[8,16]{1,0:T(8,128)} %bitcast.4, s32[9,64]{1,0:T(8,128)} %get-tuple-element.13.codes, bf16[32,16,256]{2,1,0:T(8,128)(2,1)} %collective-permute-done.inner, bf16[32,16,256]{2,1,0:T(8,128)(2,1)} %collective-permute-done.1.outer, ...), custom_call_target="tpu_custom_call" | custom-call | flops 40000000000 | tf_op jit(solution)/shard_map/local/pallas_call | solution.py:347
  40.2 0.0 collective-permute-done.4
  40.2 0.0 collective-permute-done.5
  40.2 2.5 %add_convert_fusion = bf16[64,16,256]{2,1,0:T(8,128)(2,1)} fusion(bf16[64,16,256]{2,1,0:T(8,128)(2,1)} %collective-permute-done.5, f32[64,16,256]{2,1,0:T(8,128)} %local.1, bf16[64,16,256]{2,1,0:T(8,128)(2,1)} %collective-permute-done.4), kind=kLoop, calls=%fused_computation | loop fusion | flops 1310720 | bytes 2621440 | tf_op jit(solution)/shard_map/convert_element_type | solution.py:413
Async XLA Ops:
  0.0 21.5 %collective-permute-start.3 = (bf16[64,16,256]{2,1,0:T(8,128)(2,1)}, bf16[64,16,256]{2,1,0:T(8,128)(2,1)}, u32[]{:S(2)}, u32[]{:S(2)}) collective-permute-start(bf16[64,16,256]{2,1,0:T(8,128)(2,1)} %own_src.3), channel_id=1, source_target_pairs={{0,3},{1,0},{2,1},{3,2},{4,7},{5,4},{6,5},{7,6},{8,11},{9,8},{10,9... | collective-permute-start | bytes 1572872 | tf_op jit(solution)/shard_map/ppermute | solution.py:380
  3.3 18.2 %collective-permute-start.2 = (bf16[64,16,256]{2,1,0:T(8,128)(2,1)}, bf16[64,16,256]{2,1,0:T(8,128)(2,1)}, u32[]{:S(2)}, u32[]{:S(2)}) collective-permute-start(bf16[64,16,256]{2,1,0:T(8,128)(2,1)} %own_src.3), channel_id=1, source_target_pairs={{0,1},{1,2},{2,3},{3,0},{4,5},{5,6},{6,7},{7,4},{8,9},{9,10},{10,1... | collective-permute-start | bytes 1572872 | tf_op jit(solution)/shard_map/ppermute | solution.py:380
  8.5 13.0 %collective-permute-start = (bf16[32,16,256]{2,1,0:T(8,128)(2,1)}, bf16[32,16,256]{2,1,0:T(8,128)(2,1)}, u32[]{:S(2)}, u32[]{:S(2)}) collective-permute-start(bf16[32,16,256]{2,1,0:T(8,128)(2,1)} %get-tuple-element.11), channel_id=1, source_target_pairs={{0,4},{4,0},{8,12},{12,8},{16,20},{20,16},{24,28},{28,24},{32,36},... | collective-permute-start | bytes 786440 | tf_op jit(solution)/shard_map/ppermute | solution.py:385
  9.5 12.0 %collective-permute-start.1 = (bf16[32,16,256]{2,1,0:T(8,128)(2,1)}, bf16[32,16,256]{2,1,0:T(8,128)(2,1)}, u32[]{:S(2)}, u32[]{:S(2)}) collective-permute-start(bf16[32,16,256]{2,1,0:T(8,128)(2,1)} %get-tuple-element.12), channel_id=1, source_target_pairs={{0,124},{4,8},{8,4},{12,16},{16,12},{20,24},{24,20},{28,32},{32,28... | collective-permute-start | bytes 786440 | tf_op jit(solution)/shard_map/ppermute | solution.py:385
  11.1 21.3 %all-to-all-start = ((bf16[128,8,128]{2,1,0:T(8,128)(2,1)}), bf16[128,8,128]{2,1,0:T(8,128)(2,1)}, u32[]{:S(2)}, u32[]{:S(2)}) async-start(bf16[128,8,128]{2,1,0:T(8,128)(2,1)} %get-tuple-element.14), calls=%async_computation | async-start | bytes 524288 | tf_op jit(solution)/shard_map/all_to_all | solution.py:403
  26.8 13.4 %collective-permute-start.4 = (bf16[64,16,256]{2,1,0:T(8,128)(2,1)}, bf16[64,16,256]{2,1,0:T(8,128)(2,1)}, u32[]{:S(2)}, u32[]{:S(2)}) collective-permute-start(bf16[64,16,256]{2,1,0:T(8,128)(2,1)} %get-tuple-element.15), channel_id=1, source_target_pairs={{0,4},{4,0},{8,12},{12,8},{16,20},{20,16},{24,28},{28,24},{32,36},... | collective-permute-start | bytes 1572872 | tf_op jit(solution)/shard_map/ppermute | solution.py:385
  28.0 12.2 %collective-permute-start.5 = (bf16[64,16,256]{2,1,0:T(8,128)(2,1)}, bf16[64,16,256]{2,1,0:T(8,128)(2,1)}, u32[]{:S(2)}, u32[]{:S(2)}) collective-permute-start(bf16[64,16,256]{2,1,0:T(8,128)(2,1)} %get-tuple-element.16), channel_id=1, source_target_pairs={{0,124},{4,8},{8,4},{12,16},{16,12},{20,24},{24,20},{28,32},{32,28... | collective-permute-start | bytes 1572872 | tf_op jit(solution)/shard_map/ppermute | solution.py:385

commit v3 on v2

--- a/solution.py
+++ b/solution.py
@@ -71,7 +71,7 @@
     count, rhs, points = src.shape
     rank = basis.shape[1]
     sections = total.shape[0]
-    chunks = 4
+    chunks = 2
     boxes = count // chunks
     pairs = []
     for c in range(chunks):
@@ -240,7 +240,7 @@
     leaves = lax.axis_size("leaf")
     slabs = lax.axis_size("slab")
     my_top = my_leaf // GROUP
-    chunks = 4
+    chunks = 2
     here = sections // chunks
     pairs = [(inner.at[pl.ds(0, fours)], beside.at[0]), (outer.at[pl.ds(0, fours)], beside.at[1])]
     for c in range(chunks):
@@ -282,7 +282,7 @@
         wide = jnp.concatenate(pairs, axis=1)
         coupled[q] = dot(wide, couple_w[q].reshape(link_count * rank, rank).astype(BF16))
 
-    for copy in copies[6:10]:
+    for copy in copies[4:8]:
         copy.wait()
 
     def store(at, many, total):
@@ -290,7 +290,7 @@
 
     near_sum(lambda j, b: codes[j, b], table, near_w, store)
 
-    for copy in copies[10:13]:
+    for copy in copies[8:11]:
         copy.wait()
     slab_tops = top_links.shape[0]
     half = rhs // 2
@@ -311,7 +311,7 @@
         tables[0, q], tables[1, q] = split(jnp.concatenate([value, zero], axis=1))
         tables[2, q], tables[3, q] = split(jnp.concatenate([zero, value], axis=1))
 
-    for copy in copies[13:]:
+    for copy in copies[11:]:
         copy.wait()
     mask = own_mask(rhs, rank)
     none = jnp.zeros((rhs, 2 * rank), BF16)
@@ -364,9 +364,9 @@
             pltpu.VMEM((sections, rhs, rank), F32),
             pltpu.VMEM((4, sections, rhs, 2 * rank), BF16),
             pltpu.VMEM((count // 4, 4 * rhs, 4 * rank), BF16),
-            pltpu.SemaphoreType.DMA((15,)),
+            pltpu.SemaphoreType.DMA((13,)),
         ],
-        compiler_params=params(),
+        compiler_params=params(56),
         cost_estimate=cost(40),
         name="local",
     )(

time: 43 us -> 42.7 us (level)
  no operation moved by 1% of the time
where the time goes in v3:
time: 42.7 us; the launch traced here: 42.4 us
  starting transfers between devices  18.3 us (43%)
  Pallas kernels  18.1 us (42%)
  waiting for transfers between devices  3.68 us (9%)
  other arithmetic  2.24 us (5%)
    all_to_all x1, starting transfers between devices, shards(): tops = lax.all_to_all(sent, ('leaf', 'slab'), 0, 0, tiled=True)  10.3 us
    pallas_call x1, Pallas kernels, local_call(): pl.pallas_call(local_kernel, in_specs=[SMEM] * 4 + [HBM] * 12, out_specs=...  7.72 us
    pallas_call x1, Pallas kernels, beside_call(): pl.pallas_call(beside_kernel, in_specs=[HBM] * 7, out_specs=[VMEM] * 3, o...  5.27 us
    pallas_call x1, Pallas kernels, moments_call(): pl.pallas_call(moments_kernel, in_specs=[SMEM, HBM, HBM, HBM, HBM, HBM],...  5.12 us
    ppermute x4, starting transfers between devices, swapped(): lax.ppermute(x, 'leaf', [(i, (i + (1 if i % 2 == first else -1)) % count)...  4.64 us
    all_to_all x1, waiting for transfers between devices, shards(): tops = lax.all_to_all(sent, ('leaf', 'slab'), 0, 0, tiled=True)  3.67 us
    ppermute x2, starting transfers between devices, shifted(): lax.ppermute(x, axis, [(i, (i + step) % count) for i in range(count)])  3.31 us
    convert_element_type x1, other arithmetic, shards(): (local + near_inner.astype(F32) + near_outer.astype(F32)).astype(BF16)  2.24 us
  transfers between devices with their start and end apart: 7, of which 1 were waited for; matrix products, arithmetic and copies ran while one was open for 0% of the time, Pallas kernels for 43%

profile of v3, /device:TPU:1, one launch (start us, length us, event | category | flops | bytes accessed | tf_op | source)
XLA Modules:
  0.0 42.4 jit_solution(7194246592736200908)
XLA Ops:
  0.0 3.3 %collective-permute-start.3 = (bf16[64,16,256]{2,1,0:T(8,128)(2,1)}, bf16[64,16,256]{2,1,0:T(8,128)(2,1)}, u32[]{:S(2)}, u32[]{:S(2)}) collective-permute-start(bf16[64,16,256]{2,1,0:T(8,128)(2,1)} %own_src.3), channel_id=1, source_target_pairs={{0,3},{1,0},{2,1},{3,2},{4,7},{5,4},{6,5},{7,6},{8,11},{9,8},{10,9... | collective-permute-start | bytes 1572872 | tf_op jit(solution)/shard_map/ppermute | solution.py:380
  3.3 0.0 collective-permute-start.2
  3.3 5.1 %moments.1 = (bf16[32,16,256]{2,1,0:T(8,128)(2,1)}, bf16[32,16,256]{2,1,0:T(8,128)(2,1)}, bf16[128,8,128]{2,1,0:T(8,128)(2,1)}) custom-call(s32[64]{0:T(128)} %parent.3, bf16[64,16,256]{2,1,0:T(8,128)(2,1)} %own_src.3, bf16[64,64,256]{2,1,0:T(8,128)(2,1)} %source_basis.1, f32[64,64,64]{2,1,0:T(8,128)} %up_leaf.1, f32[16,64,64]{2,1,0:T(8,128)} %up_section.1, ...), custom_call_target="tpu_custom_call" | custom-call | tf_op jit(solution)/shard_map/moments/pallas_call | solution.py:135
  8.4 1.0 %collective-permute-start = (bf16[32,16,256]{2,1,0:T(8,128)(2,1)}, bf16[32,16,256]{2,1,0:T(8,128)(2,1)}, u32[]{:S(2)}, u32[]{:S(2)}) collective-permute-start(bf16[32,16,256]{2,1,0:T(8,128)(2,1)} %get-tuple-element.11), channel_id=1, source_target_pairs={{0,4},{4,0},{8,12},{12,8},{16,20},{20,16},{24,28},{28,24},{32,36},... | collective-permute-start | bytes 786440 | tf_op jit(solution)/shard_map/ppermute | solution.py:385
  9.5 1.6 %collective-permute-start.1 = (bf16[32,16,256]{2,1,0:T(8,128)(2,1)}, bf16[32,16,256]{2,1,0:T(8,128)(2,1)}, u32[]{:S(2)}, u32[]{:S(2)}) collective-permute-start(bf16[32,16,256]{2,1,0:T(8,128)(2,1)} %get-tuple-element.12), channel_id=1, source_target_pairs={{0,124},{4,8},{8,4},{12,16},{16,12},{20,24},{24,20},{28,32},{32,28... | collective-permute-start | bytes 786440 | tf_op jit(solution)/shard_map/ppermute | solution.py:385
  11.1 10.3 %all-to-all-start = ((bf16[128,8,128]{2,1,0:T(8,128)(2,1)}), bf16[128,8,128]{2,1,0:T(8,128)(2,1)}, u32[]{:S(2)}, u32[]{:S(2)}) async-start(bf16[128,8,128]{2,1,0:T(8,128)(2,1)} %get-tuple-element.14), calls=%async_computation | async-start | bytes 524288 | tf_op jit(solution)/shard_map/all_to_all | solution.py:403
  21.4 0.0 collective-permute-done.inner
  21.4 0.0 collective-permute-done.1.outer
  21.4 0.0 collective-permute-done.3.from_high
  21.4 0.0 collective-permute-done.2.from_low
  21.5 5.3 %beside.1 = (bf16[64,16,256]{2,1,0:T(8,128)(2,1)}, bf16[64,16,256]{2,1,0:T(8,128)(2,1)}, s32[9,64]{1,0:T(8,128)}) custom-call(bf16[32,16,256]{2,1,0:T(8,128)(2,1)} %collective-permute-done.inner, bf16[32,16,256]{2,1,0:T(8,128)(2,1)} %collective-permute-done.1.outer, bf16[64,16,256]{2,1,0:T(8,128)(2,1)} %collective-permute-done.2.from_low, ...), custom_call_target="tpu_custom_call" | custom-call | tf_op jit(solution)/shard_map/beside/pallas_call | solution.py:207
  26.7 1.2 %collective-permute-start.4 = (bf16[64,16,256]{2,1,0:T(8,128)(2,1)}, bf16[64,16,256]{2,1,0:T(8,128)(2,1)S(1)}, u32[]{:S(2)}, u32[]{:S(2)}) collective-permute-start(bf16[64,16,256]{2,1,0:T(8,128)(2,1)} %get-tuple-element.15), channel_id=1, source_target_pairs={{0,4},{4,0},{8,12},{12,8},{16,20},{20,16},{24,28},{28,24},{32,36},... | collective-permute-start | bytes 1572872 | tf_op jit(solution)/shard_map/ppermute | solution.py:385
  28.0 0.8 %collective-permute-start.5 = (bf16[64,16,256]{2,1,0:T(8,128)(2,1)}, bf16[64,16,256]{2,1,0:T(8,128)(2,1)S(1)}, u32[]{:S(2)}, u32[]{:S(2)}) collective-permute-start(bf16[64,16,256]{2,1,0:T(8,128)(2,1)} %get-tuple-element.16), channel_id=1, source_target_pairs={{0,124},{4,8},{8,4},{12,16},{16,12},{20,24},{24,20},{28,32},{32,28... | collective-permute-start | bytes 1572872 | tf_op jit(solution)/shard_map/ppermute | solution.py:385
  28.7 3.7 %all-to-all-done.tops = bf16[128,8,128]{2,1,0:T(8,128)(2,1)} async-done(((bf16[128,8,128]{2,1,0:T(8,128)(2,1)}), bf16[128,8,128]{2,1,0:T(8,128)(2,1)}, u32[]{:S(2)}, u32[]{:S(2)}) %all-to-all-start) | async-done | bytes 262176 | tf_op jit(solution)/shard_map/all_to_all | solution.py:403
  32.4 7.7 %local.1 = f32[64,16,256]{2,1,0:T(8,128)} custom-call(s32[64]{0:T(128)} %parent.3, s32[8,8]{1,0:T(8,128)} %top_links.1, s32[8,16]{1,0:T(8,128)} %bitcast.4, s32[9,64]{1,0:T(8,128)} %get-tuple-element.13.codes, bf16[32,16,256]{2,1,0:T(8,128)(2,1)} %collective-permute-done.inner, bf16[32,16,256]{2,1,0:T(8,128)(2,1)} %collective-permute-done.1.outer, ...), custom_call_target="tpu_custom_call" | custom-call | flops 40000000000 | tf_op jit(solution)/shard_map/local/pallas_call | solution.py:347
  40.1 0.0 collective-permute-done.4
  40.1 0.0 collective-permute-done.5
  40.1 2.2 %add_convert_fusion = bf16[64,16,256]{2,1,0:T(8,128)(2,1)} fusion(bf16[64,16,256]{2,1,0:T(8,128)(2,1)S(1)} %collective-permute-done.5, f32[64,16,256]{2,1,0:T(8,128)} %local.1, bf16[64,16,256]{2,1,0:T(8,128)(2,1)S(1)} %collective-permute-done.4), kind=kLoop, calls=%fused_computation | loop fusion | flops 1310720 | bytes 2621440 | tf_op jit(solution)/shard_map/convert_element_type | solution.py:413
Async XLA Ops:
  0.0 21.4 %collective-permute-start.3 = (bf16[64,16,256]{2,1,0:T(8,128)(2,1)}, bf16[64,16,256]{2,1,0:T(8,128)(2,1)}, u32[]{:S(2)}, u32[]{:S(2)}) collective-permute-start(bf16[64,16,256]{2,1,0:T(8,128)(2,1)} %own_src.3), channel_id=1, source_target_pairs={{0,3},{1,0},{2,1},{3,2},{4,7},{5,4},{6,5},{7,6},{8,11},{9,8},{10,9... | collective-permute-start | bytes 1572872 | tf_op jit(solution)/shard_map/ppermute | solution.py:380
  3.3 18.1 %collective-permute-start.2 = (bf16[64,16,256]{2,1,0:T(8,128)(2,1)}, bf16[64,16,256]{2,1,0:T(8,128)(2,1)}, u32[]{:S(2)}, u32[]{:S(2)}) collective-permute-start(bf16[64,16,256]{2,1,0:T(8,128)(2,1)} %own_src.3), channel_id=1, source_target_pairs={{0,1},{1,2},{2,3},{3,0},{4,5},{5,6},{6,7},{7,4},{8,9},{9,10},{10,1... | collective-permute-start | bytes 1572872 | tf_op jit(solution)/shard_map/ppermute | solution.py:380
  8.4 13.0 %collective-permute-start = (bf16[32,16,256]{2,1,0:T(8,128)(2,1)}, bf16[32,16,256]{2,1,0:T(8,128)(2,1)}, u32[]{:S(2)}, u32[]{:S(2)}) collective-permute-start(bf16[32,16,256]{2,1,0:T(8,128)(2,1)} %get-tuple-element.11), channel_id=1, source_target_pairs={{0,4},{4,0},{8,12},{12,8},{16,20},{20,16},{24,28},{28,24},{32,36},... | collective-permute-start | bytes 786440 | tf_op jit(solution)/shard_map/ppermute | solution.py:385
  9.5 12.0 %collective-permute-start.1 = (bf16[32,16,256]{2,1,0:T(8,128)(2,1)}, bf16[32,16,256]{2,1,0:T(8,128)(2,1)}, u32[]{:S(2)}, u32[]{:S(2)}) collective-permute-start(bf16[32,16,256]{2,1,0:T(8,128)(2,1)} %get-tuple-element.12), channel_id=1, source_target_pairs={{0,124},{4,8},{8,4},{12,16},{16,12},{20,24},{24,20},{28,32},{32,28... | collective-permute-start | bytes 786440 | tf_op jit(solution)/shard_map/ppermute | solution.py:385
  11.1 21.3 %all-to-all-start = ((bf16[128,8,128]{2,1,0:T(8,128)(2,1)}), bf16[128,8,128]{2,1,0:T(8,128)(2,1)}, u32[]{:S(2)}, u32[]{:S(2)}) async-start(bf16[128,8,128]{2,1,0:T(8,128)(2,1)} %get-tuple-element.14), calls=%async_computation | async-start | bytes 524288 | tf_op jit(solution)/shard_map/all_to_all | solution.py:403
  26.7 13.4 %collective-permute-start.4 = (bf16[64,16,256]{2,1,0:T(8,128)(2,1)}, bf16[64,16,256]{2,1,0:T(8,128)(2,1)S(1)}, u32[]{:S(2)}, u32[]{:S(2)}) collective-permute-start(bf16[64,16,256]{2,1,0:T(8,128)(2,1)} %get-tuple-element.15), channel_id=1, source_target_pairs={{0,4},{4,0},{8,12},{12,8},{16,20},{20,16},{24,28},{28,24},{32,36},... | collective-permute-start | bytes 1572872 | tf_op jit(solution)/shard_map/ppermute | solution.py:385
  28.0 12.2 %collective-permute-start.5 = (bf16[64,16,256]{2,1,0:T(8,128)(2,1)}, bf16[64,16,256]{2,1,0:T(8,128)(2,1)S(1)}, u32[]{:S(2)}, u32[]{:S(2)}) collective-permute-start(bf16[64,16,256]{2,1,0:T(8,128)(2,1)} %get-tuple-element.16), channel_id=1, source_target_pairs={{0,124},{4,8},{8,4},{12,16},{16,12},{20,24},{24,20},{28,32},{32,28... | collective-permute-start | bytes 1572872 | tf_op jit(solution)/shard_map/ppermute | solution.py:385

commit v4 on v3

--- a/solution.py
+++ b/solution.py
@@ -111,8 +111,8 @@
     fours = sections // 4
     for four in range(fours):
         wide = jnp.concatenate([total[4 * four + one] for one in range(4)], axis=1)
-        to_inner[four] = wide.astype(BF16)
-        to_outer[four] = wide.astype(BF16)
+        for ref in (to_inner, to_outer):
+            ref[four], ref[LISTS + 1 + four] = split(wide)
         term = dot_split(wide, raise_[4 * four : 4 * four + 4].reshape(4 * rank, rank))
         partial = term if four == 0 else partial + term
     half = rhs // 2
@@ -240,17 +240,20 @@
     leaves = lax.axis_size("leaf")
     slabs = lax.axis_size("slab")
     my_top = my_leaf // GROUP
+    parts = pl.ds(0, LISTS + 1 + fours)
     chunks = 2
     here = sections // chunks
-    pairs = [(inner.at[pl.ds(0, fours)], beside.at[0]), (outer.at[pl.ds(0, fours)], beside.at[1])]
+    pairs = [
+        (near_blocks, near_w),
+        (from_low, table.at[pl.ds(0, count)]),
+        (own_src, table.at[pl.ds(count, count)]),
+        (from_high, table.at[pl.ds(2 * count, count)]),
+        (inner.at[parts], beside.at[0]), (outer.at[parts], beside.at[1]),
+    ]
     for c in range(chunks):
         at = pl.ds(c * here, here)
         pairs.append((coupling.at[at], couple_w.at[at]))
     pairs += [
-        (near_blocks, near_w),
-        (from_low, table.at[pl.ds(0, count)]),
-        (own_src, table.at[pl.ds(count, count)]),
-        (from_high, table.at[pl.ds(2 * count, count)]),
         (tops, tops_v), (couplers.at[my_top], coupler), (down_section, section_w),
         (down_leaf, leaf_w), (target, target_w),
     ]
@@ -258,17 +261,26 @@
 
     table[3 * count] = jnp.zeros((rhs, points), BF16)
 
-    for copy in copies[:2]:
+    for copy in copies[:4]:
+        copy.wait()
+
+    def store(at, many, total):
+        out[pl.ds(at, many)] = total.reshape(many, rhs, points)
+
+    near_sum(lambda j, b: codes[j, b], table, near_w, store)
+
+    for copy in copies[4:6]:
         copy.wait()
     zero = jnp.zeros((rhs, rank), F32)
     for side in range(2):
-        for four in range(fours):
-            wide = beside[side, four].astype(F32)
-            for one in range(4):
-                value = wide[:, one * rank : (one + 1) * rank]
-                at = side * sections + 4 * four + one
-                left[at] = jnp.concatenate([value, zero], axis=1).astype(BF16)
-                right[at] = jnp.concatenate([zero, value], axis=1).astype(BF16)
+        for part in range(2):
+            for four in range(fours):
+                wide = beside[side, part * (LISTS + 1) + four].astype(F32)
+                for one in range(4):
+                    value = wide[:, one * rank : (one + 1) * rank]
+                    at = side * sections + 4 * four + one
+                    left[part, at] = jnp.concatenate([value, zero], axis=1).astype(BF16)
+                    right[part, at] = jnp.concatenate([zero, value], axis=1).astype(BF16)
 
     def slot(j, q):
         entry = links[j, q]
@@ -277,18 +289,15 @@
 
     for q in range(sections):
         if q % here == 0:
-            copies[2 + q // here].wait()
-        pairs = [left[slot(j, q)] + right[slot(j + 1, q)] for j in range(0, link_count, 2)]
-        wide = jnp.concatenate(pairs, axis=1)
-        coupled[q] = dot(wide, couple_w[q].reshape(link_count * rank, rank).astype(BF16))
-
-    for copy in copies[4:8]:
-        copy.wait()
-
-    def store(at, many, total):
-        out[pl.ds(at, many)] = total.reshape(many, rhs, points)
-
-    near_sum(lambda j, b: codes[j, b], table, near_w, store)
+            copies[6 + q // here].wait()
+        slots = [slot(j, q) for j in range(link_count)]
+        lines = []
+        for part in range(2):
+            pairs = [left[part, slots[j]] + right[part, slots[j + 1]] for j in range(0, link_count, 2)]
+            lines.append(jnp.concatenate(pairs, axis=1))
+        weights = couple_w[q].reshape(link_count * rank, rank).astype(BF16)
+        both = dot(jnp.concatenate(lines, axis=0), weights)
+        coupled[q] = both[:rhs] + both[rhs:]
 
     for copy in copies[8:11]:
         copy.wait()
@@ -352,15 +361,15 @@
         scratch_shapes=[
             pltpu.VMEM((3 * count + 1, rhs, points), BF16),
             pltpu.VMEM(near_blocks.shape, BF16),
-            pltpu.VMEM((2, sections // 4, rhs, points), BF16),
+            pltpu.VMEM((2, LISTS + 1 + sections // 4, rhs, points), BF16),
             pltpu.VMEM(coupling.shape, F32),
             pltpu.VMEM(tops.shape, BF16),
             pltpu.VMEM(couplers.shape[1:], F32),
             pltpu.VMEM(down_section.shape, F32),
             pltpu.VMEM(down_leaf.shape, F32),
             pltpu.VMEM(target.shape, BF16),
-            pltpu.VMEM((2 * sections, rhs, 2 * rank), BF16),
-            pltpu.VMEM((2 * sections, rhs, 2 * rank), BF16),
+            pltpu.VMEM((2, 2 * sections, rhs, 2 * rank), BF16),
+            pltpu.VMEM((2, 2 * sections, rhs, 2 * rank), BF16),
             pltpu.VMEM((sections, rhs, rank), F32),
             pltpu.VMEM((4, sections, rhs, 2 * rank), BF16),
             pltpu.VMEM((count // 4, 4 * rhs, 4 * rank), BF16),

time: 42.7 us -> 42.6 us (level)
  no operation moved by 1% of the time
where the time goes in v4:
time: 42.6 us; the launch traced here: 42.3 us
  starting transfers between devices  18.3 us (43%)
  Pallas kernels  18 us (42%)
  waiting for transfers between devices  3.68 us (9%)
  other arithmetic  2.24 us (5%)
    all_to_all x1, starting transfers between devices, shards(): tops = lax.all_to_all(sent, ('leaf', 'slab'), 0, 0, tiled=True)  10.3 us
    pallas_call x1, Pallas kernels, local_call(): pl.pallas_call(local_kernel, in_specs=[SMEM] * 4 + [HBM] * 12, out_specs=...  7.65 us
    pallas_call x1, Pallas kernels, beside_call(): pl.pallas_call(beside_kernel, in_specs=[HBM] * 7, out_specs=[VMEM] * 3, o...  5.27 us
    pallas_call x1, Pallas kernels, moments_call(): pl.pallas_call(moments_kernel, in_specs=[SMEM, HBM, HBM, HBM, HBM, HBM],...  5.12 us
    ppermute x4, starting transfers between devices, swapped(): lax.ppermute(x, 'leaf', [(i, (i + (1 if i % 2 == first else -1)) % count)...  4.63 us
    all_to_all x1, waiting for transfers between devices, shards(): tops = lax.all_to_all(sent, ('leaf', 'slab'), 0, 0, tiled=True)  3.67 us
    ppermute x2, starting transfers between devices, shifted(): lax.ppermute(x, axis, [(i, (i + step) % count) for i in range(count)])  3.31 us
    convert_element_type x1, other arithmetic, shards(): (local + near_inner.astype(F32) + near_outer.astype(F32)).astype(BF16)  2.24 us
  transfers between devices with their start and end apart: 7, of which 1 were waited for; matrix products, arithmetic and copies ran while one was open for 0% of the time, Pallas kernels for 43%

profile of v4, /device:TPU:1, one launch (start us, length us, event | category | flops | bytes accessed | tf_op | source)
XLA Modules:
  0.0 42.3 jit_solution(18303767580553174102)
XLA Ops:
  0.0 3.3 %collective-permute-start.3 = (bf16[64,16,256]{2,1,0:T(8,128)(2,1)}, bf16[64,16,256]{2,1,0:T(8,128)(2,1)}, u32[]{:S(2)}, u32[]{:S(2)}) collective-permute-start(bf16[64,16,256]{2,1,0:T(8,128)(2,1)} %own_src.3), channel_id=1, source_target_pairs={{0,3},{1,0},{2,1},{3,2},{4,7},{5,4},{6,5},{7,6},{8,11},{9,8},{10,9... | collective-permute-start | bytes 1572872 | tf_op jit(solution)/shard_map/ppermute | solution.py:389
  3.3 0.0 collective-permute-start.2
  3.3 5.1 %moments.1 = (bf16[32,16,256]{2,1,0:T(8,128)(2,1)}, bf16[32,16,256]{2,1,0:T(8,128)(2,1)}, bf16[128,8,128]{2,1,0:T(8,128)(2,1)}) custom-call(s32[64]{0:T(128)} %parent.3, bf16[64,16,256]{2,1,0:T(8,128)(2,1)} %own_src.3, bf16[64,64,256]{2,1,0:T(8,128)(2,1)} %source_basis.1, f32[64,64,64]{2,1,0:T(8,128)} %up_leaf.1, f32[16,64,64]{2,1,0:T(8,128)} %up_section.1, ...), custom_call_target="tpu_custom_call" | custom-call | tf_op jit(solution)/shard_map/moments/pallas_call | solution.py:135
  8.4 1.0 %collective-permute-start = (bf16[32,16,256]{2,1,0:T(8,128)(2,1)}, bf16[32,16,256]{2,1,0:T(8,128)(2,1)}, u32[]{:S(2)}, u32[]{:S(2)}) collective-permute-start(bf16[32,16,256]{2,1,0:T(8,128)(2,1)} %get-tuple-element.11), channel_id=1, source_target_pairs={{0,4},{4,0},{8,12},{12,8},{16,20},{20,16},{24,28},{28,24},{32,36},... | collective-permute-start | bytes 786440 | tf_op jit(solution)/shard_map/ppermute | solution.py:394
  9.5 1.6 %collective-permute-start.1 = (bf16[32,16,256]{2,1,0:T(8,128)(2,1)}, bf16[32,16,256]{2,1,0:T(8,128)(2,1)}, u32[]{:S(2)}, u32[]{:S(2)}) collective-permute-start(bf16[32,16,256]{2,1,0:T(8,128)(2,1)} %get-tuple-element.12), channel_id=1, source_target_pairs={{0,124},{4,8},{8,4},{12,16},{16,12},{20,24},{24,20},{28,32},{32,28... | collective-permute-start | bytes 786440 | tf_op jit(solution)/shard_map/ppermute | solution.py:394
  11.1 10.3 %all-to-all-start = ((bf16[128,8,128]{2,1,0:T(8,128)(2,1)}), bf16[128,8,128]{2,1,0:T(8,128)(2,1)}, u32[]{:S(2)}, u32[]{:S(2)}) async-start(bf16[128,8,128]{2,1,0:T(8,128)(2,1)} %get-tuple-element.14), calls=%async_computation | async-start | bytes 524288 | tf_op jit(solution)/shard_map/all_to_all | solution.py:412
  21.4 0.0 collective-permute-done.inner
  21.4 0.0 collective-permute-done.1.outer
  21.4 0.0 collective-permute-done.3.from_high
  21.5 0.0 collective-permute-done.2.from_low
  21.5 5.3 %beside.1 = (bf16[64,16,256]{2,1,0:T(8,128)(2,1)}, bf16[64,16,256]{2,1,0:T(8,128)(2,1)}, s32[9,64]{1,0:T(8,128)}) custom-call(bf16[32,16,256]{2,1,0:T(8,128)(2,1)} %collective-permute-done.inner, bf16[32,16,256]{2,1,0:T(8,128)(2,1)} %collective-permute-done.1.outer, bf16[64,16,256]{2,1,0:T(8,128)(2,1)} %collective-permute-done.2.from_low, ...), custom_call_target="tpu_custom_call" | custom-call | tf_op jit(solution)/shard_map/beside/pallas_call | solution.py:207
  26.7 1.2 %collective-permute-start.4 = (bf16[64,16,256]{2,1,0:T(8,128)(2,1)}, bf16[64,16,256]{2,1,0:T(8,128)(2,1)S(1)}, u32[]{:S(2)}, u32[]{:S(2)}) collective-permute-start(bf16[64,16,256]{2,1,0:T(8,128)(2,1)} %get-tuple-element.15), channel_id=1, source_target_pairs={{0,4},{4,0},{8,12},{12,8},{16,20},{20,16},{24,28},{28,24},{32,36},... | collective-permute-start | bytes 1572872 | tf_op jit(solution)/shard_map/ppermute | solution.py:394
  28.0 0.8 %collective-permute-start.5 = (bf16[64,16,256]{2,1,0:T(8,128)(2,1)}, bf16[64,16,256]{2,1,0:T(8,128)(2,1)S(1)}, u32[]{:S(2)}, u32[]{:S(2)}) collective-permute-start(bf16[64,16,256]{2,1,0:T(8,128)(2,1)} %get-tuple-element.16), channel_id=1, source_target_pairs={{0,124},{4,8},{8,4},{12,16},{16,12},{20,24},{24,20},{28,32},{32,28... | collective-permute-start | bytes 1572872 | tf_op jit(solution)/shard_map/ppermute | solution.py:394
  28.7 3.7 %all-to-all-done.tops = bf16[128,8,128]{2,1,0:T(8,128)(2,1)} async-done(((bf16[128,8,128]{2,1,0:T(8,128)(2,1)}), bf16[128,8,128]{2,1,0:T(8,128)(2,1)}, u32[]{:S(2)}, u32[]{:S(2)}) %all-to-all-start) | async-done | bytes 262176 | tf_op jit(solution)/shard_map/all_to_all | solution.py:412
  32.4 7.7 %local.1 = f32[64,16,256]{2,1,0:T(8,128)} custom-call(s32[64]{0:T(128)} %parent.3, s32[8,8]{1,0:T(8,128)} %top_links.1, s32[8,16]{1,0:T(8,128)} %bitcast.4, s32[9,64]{1,0:T(8,128)} %get-tuple-element.13.codes, bf16[32,16,256]{2,1,0:T(8,128)(2,1)} %collective-permute-done.inner, bf16[32,16,256]{2,1,0:T(8,128)(2,1)} %collective-permute-done.1.outer, ...), custom_call_target="tpu_custom_call" | custom-call | flops 40000000000 | tf_op jit(solution)/shard_map/local/pallas_call | solution.py:356
  40.1 0.0 collective-permute-done.4
  40.1 0.0 collective-permute-done.5
  40.1 2.2 %add_convert_fusion = bf16[64,16,256]{2,1,0:T(8,128)(2,1)} fusion(bf16[64,16,256]{2,1,0:T(8,128)(2,1)S(1)} %collective-permute-done.5, f32[64,16,256]{2,1,0:T(8,128)} %local.1, bf16[64,16,256]{2,1,0:T(8,128)(2,1)S(1)} %collective-permute-done.4), kind=kLoop, calls=%fused_computation | loop fusion | flops 1310720 | bytes 2621440 | tf_op jit(solution)/shard_map/convert_element_type | solution.py:422
Async XLA Ops:
  0.0 21.4 %collective-permute-start.3 = (bf16[64,16,256]{2,1,0:T(8,128)(2,1)}, bf16[64,16,256]{2,1,0:T(8,128)(2,1)}, u32[]{:S(2)}, u32[]{:S(2)}) collective-permute-start(bf16[64,16,256]{2,1,0:T(8,128)(2,1)} %own_src.3), channel_id=1, source_target_pairs={{0,3},{1,0},{2,1},{3,2},{4,7},{5,4},{6,5},{7,6},{8,11},{9,8},{10,9... | collective-permute-start | bytes 1572872 | tf_op jit(solution)/shard_map/ppermute | solution.py:389
  3.3 18.1 %collective-permute-start.2 = (bf16[64,16,256]{2,1,0:T(8,128)(2,1)}, bf16[64,16,256]{2,1,0:T(8,128)(2,1)}, u32[]{:S(2)}, u32[]{:S(2)}) collective-permute-start(bf16[64,16,256]{2,1,0:T(8,128)(2,1)} %own_src.3), channel_id=1, source_target_pairs={{0,1},{1,2},{2,3},{3,0},{4,5},{5,6},{6,7},{7,4},{8,9},{9,10},{10,1... | collective-permute-start | bytes 1572872 | tf_op jit(solution)/shard_map/ppermute | solution.py:389
  8.4 13.0 %collective-permute-start = (bf16[32,16,256]{2,1,0:T(8,128)(2,1)}, bf16[32,16,256]{2,1,0:T(8,128)(2,1)}, u32[]{:S(2)}, u32[]{:S(2)}) collective-permute-start(bf16[32,16,256]{2,1,0:T(8,128)(2,1)} %get-tuple-element.11), channel_id=1, source_target_pairs={{0,4},{4,0},{8,12},{12,8},{16,20},{20,16},{24,28},{28,24},{32,36},... | collective-permute-start | bytes 786440 | tf_op jit(solution)/shard_map/ppermute | solution.py:394
  9.5 12.0 %collective-permute-start.1 = (bf16[32,16,256]{2,1,0:T(8,128)(2,1)}, bf16[32,16,256]{2,1,0:T(8,128)(2,1)}, u32[]{:S(2)}, u32[]{:S(2)}) collective-permute-start(bf16[32,16,256]{2,1,0:T(8,128)(2,1)} %get-tuple-element.12), channel_id=1, source_target_pairs={{0,124},{4,8},{8,4},{12,16},{16,12},{20,24},{24,20},{28,32},{32,28... | collective-permute-start | bytes 786440 | tf_op jit(solution)/shard_map/ppermute | solution.py:394
  11.1 21.3 %all-to-all-start = ((bf16[128,8,128]{2,1,0:T(8,128)(2,1)}), bf16[128,8,128]{2,1,0:T(8,128)(2,1)}, u32[]{:S(2)}, u32[]{:S(2)}) async-start(bf16[128,8,128]{2,1,0:T(8,128)(2,1)} %get-tuple-element.14), calls=%async_computation | async-start | bytes 524288 | tf_op jit(solution)/shard_map/all_to_all | solution.py:412
  26.7 13.3 %collective-permute-start.4 = (bf16[64,16,256]{2,1,0:T(8,128)(2,1)}, bf16[64,16,256]{2,1,0:T(8,128)(2,1)S(1)}, u32[]{:S(2)}, u32[]{:S(2)}) collective-permute-start(bf16[64,16,256]{2,1,0:T(8,128)(2,1)} %get-tuple-element.15), channel_id=1, source_target_pairs={{0,4},{4,0},{8,12},{12,8},{16,20},{20,16},{24,28},{28,24},{32,36},... | collective-permute-start | bytes 1572872 | tf_op jit(solution)/shard_map/ppermute | solution.py:394
  28.0 12.1 %collective-permute-start.5 = (bf16[64,16,256]{2,1,0:T(8,128)(2,1)}, bf16[64,16,256]{2,1,0:T(8,128)(2,1)S(1)}, u32[]{:S(2)}, u32[]{:S(2)}) collective-permute-start(bf16[64,16,256]{2,1,0:T(8,128)(2,1)} %get-tuple-element.16), channel_id=1, source_target_pairs={{0,124},{4,8},{8,4},{12,16},{16,12},{20,24},{24,20},{28,32},{32,28... | collective-permute-start | bytes 1572872 | tf_op jit(solution)/shard_map/ppermute | solution.py:394

commit v5 on v4

--- a/solution.py
+++ b/solution.py
@@ -229,7 +229,7 @@
     parent, top_links, links, codes,
     inner, outer, coupling, from_low, own_src, from_high, near_blocks, tops, couplers, down_section,
     down_leaf, target, out,
-    table, near_w, beside, couple_w, tops_v, coupler, section_w, leaf_w, target_w,
+    held, table, near_w, beside, couple_w, tops_v, coupler, section_w, leaf_w, target_w,
     left, right, coupled, tables, spread, sems,
 ):
     count, rhs, points = out.shape
@@ -241,7 +241,7 @@
     slabs = lax.axis_size("slab")
     my_top = my_leaf // GROUP
     parts = pl.ds(0, LISTS + 1 + fours)
-    chunks = 2
+    chunks = 1
     here = sections // chunks
     pairs = [
         (near_blocks, near_w),
@@ -265,7 +265,7 @@
         copy.wait()
 
     def store(at, many, total):
-        out[pl.ds(at, many)] = total.reshape(many, rhs, points)
+        held[pl.ds(at, many)] = total.reshape(many, rhs, points)
 
     near_sum(lambda j, b: codes[j, b], table, near_w, store)
 
@@ -299,7 +299,7 @@
         both = dot(jnp.concatenate(lines, axis=0), weights)
         coupled[q] = both[:rhs] + both[rhs:]
 
-    for copy in copies[8:11]:
+    for copy in copies[7:10]:
         copy.wait()
     slab_tops = top_links.shape[0]
     half = rhs // 2
@@ -320,7 +320,7 @@
         tables[0, q], tables[1, q] = split(jnp.concatenate([value, zero], axis=1))
         tables[2, q], tables[3, q] = split(jnp.concatenate([zero, value], axis=1))
 
-    for copy in copies[11:]:
+    for copy in copies[10:]:
         copy.wait()
     mask = own_mask(rhs, rank)
     none = jnp.zeros((rhs, 2 * rank), BF16)
@@ -343,7 +343,7 @@
     for four in range(count // 4):
         at = pl.ds(4 * four, 4)
         far = dot(spread[four], target_w[4 * four : 4 * four + 4].reshape(4 * rank, points))
-        out[at] += far.reshape(4, rhs, points)
+        out[at] = (held[at] + far.reshape(4, rhs, points)).astype(BF16)
 
 
 def local_call(
@@ -357,8 +357,9 @@
         local_kernel,
         in_specs=[SMEM] * 4 + [HBM] * 12,
         out_specs=VMEM,
-        out_shape=jax.ShapeDtypeStruct((count, rhs, points), F32),
+        out_shape=jax.ShapeDtypeStruct((count, rhs, points), BF16),
         scratch_shapes=[
+            pltpu.VMEM((count, rhs, points), F32),
             pltpu.VMEM((3 * count + 1, rhs, points), BF16),
             pltpu.VMEM(near_blocks.shape, BF16),
             pltpu.VMEM((2, LISTS + 1 + sections // 4, rhs, points), BF16),
@@ -419,7 +420,7 @@
         leaf_parent, top_list, section_list.T, codes, inner, outer, section_coupling, from_low, sources,
         from_high, near_blocks, tops, top_coupling, down_section, down_leaf, target_basis,
     )
-    return (local + near_inner.astype(F32) + near_outer.astype(F32)).astype(BF16)
+    return (local.astype(F32) + near_inner.astype(F32) + near_outer.astype(F32)).astype(BF16)
 
 
 def solution(mesh):

time: 42.6 us -> 42.1 us (0.988)
  transfers between devices with their start and end apart: 7 -> 7, of which waited for: 1 -> 1; matrix products, arithmetic and copies ran while one was open for 0% -> 0% of each run, Pallas kernels for 43% -> 42%
where the time goes in v5:
time: 42.1 us; the launch traced here: 41.8 us
  starting transfers between devices  18.3 us (43%)
  Pallas kernels  17.8 us (42%)
  waiting for transfers between devices  3.67 us (9%)
  other arithmetic  2.04 us (5%)
    all_to_all x1, starting transfers between devices, shards(): tops = lax.all_to_all(sent, ('leaf', 'slab'), 0, 0, tiled=True)  10.3 us
    pallas_call x1, Pallas kernels, local_call(): pl.pallas_call(local_kernel, in_specs=[SMEM] * 4 + [HBM] * 12, out_specs=...  7.35 us
    pallas_call x1, Pallas kernels, beside_call(): pl.pallas_call(beside_kernel, in_specs=[HBM] * 7, out_specs=[VMEM] * 3, o...  5.29 us
    pallas_call x1, Pallas kernels, moments_call(): pl.pallas_call(moments_kernel, in_specs=[SMEM, HBM, HBM, HBM, HBM, HBM],...  5.12 us
    ppermute x4, starting transfers between devices, swapped(): lax.ppermute(x, 'leaf', [(i, (i + (1 if i % 2 == first else -1)) % count)...  4.63 us
    all_to_all x1, waiting for transfers between devices, shards(): tops = lax.all_to_all(sent, ('leaf', 'slab'), 0, 0, tiled=True)  3.66 us
    ppermute x2, starting transfers between devices, shifted(): lax.ppermute(x, axis, [(i, (i + step) % count) for i in range(count)])  3.31 us
    convert_element_type x1, other arithmetic, shards(): (local.astype(F32) + near_inner.astype(F32) + near_outer.astype(F32)).ast...  2.04 us
  transfers between devices with their start and end apart: 7, of which 1 were waited for; matrix products, arithmetic and copies ran while one was open for 0% of the time, Pallas kernels for 42%

profile of v5, /device:TPU:1, one launch (start us, length us, event | category | flops | bytes accessed | tf_op | source)
XLA Modules:
  0.0 41.8 jit_solution(1624295089996089285)
XLA Ops:
  0.0 3.3 %collective-permute-start.3 = (bf16[64,16,256]{2,1,0:T(8,128)(2,1)}, bf16[64,16,256]{2,1,0:T(8,128)(2,1)}, u32[]{:S(2)}, u32[]{:S(2)}) collective-permute-start(bf16[64,16,256]{2,1,0:T(8,128)(2,1)} %own_src.3), channel_id=1, source_target_pairs={{0,3},{1,0},{2,1},{3,2},{4,7},{5,4},{6,5},{7,6},{8,11},{9,8},{10,9... | collective-permute-start | bytes 1572872 | tf_op jit(solution)/shard_map/ppermute | solution.py:390
  3.3 0.0 collective-permute-start.2
  3.3 5.1 %moments.1 = (bf16[32,16,256]{2,1,0:T(8,128)(2,1)}, bf16[32,16,256]{2,1,0:T(8,128)(2,1)}, bf16[128,8,128]{2,1,0:T(8,128)(2,1)}) custom-call(s32[64]{0:T(128)} %parent.3, bf16[64,16,256]{2,1,0:T(8,128)(2,1)} %own_src.3, bf16[64,64,256]{2,1,0:T(8,128)(2,1)} %source_basis.1, f32[64,64,64]{2,1,0:T(8,128)} %up_leaf.1, f32[16,64,64]{2,1,0:T(8,128)} %up_section.1, ...), custom_call_target="tpu_custom_call" | custom-call | tf_op jit(solution)/shard_map/moments/pallas_call | solution.py:135
  8.4 1.0 %collective-permute-start = (bf16[32,16,256]{2,1,0:T(8,128)(2,1)}, bf16[32,16,256]{2,1,0:T(8,128)(2,1)}, u32[]{:S(2)}, u32[]{:S(2)}) collective-permute-start(bf16[32,16,256]{2,1,0:T(8,128)(2,1)} %get-tuple-element.11), channel_id=1, source_target_pairs={{0,4},{4,0},{8,12},{12,8},{16,20},{20,16},{24,28},{28,24},{32,36},... | collective-permute-start | bytes 786440 | tf_op jit(solution)/shard_map/ppermute | solution.py:395
  9.5 1.6 %collective-permute-start.1 = (bf16[32,16,256]{2,1,0:T(8,128)(2,1)}, bf16[32,16,256]{2,1,0:T(8,128)(2,1)}, u32[]{:S(2)}, u32[]{:S(2)}) collective-permute-start(bf16[32,16,256]{2,1,0:T(8,128)(2,1)} %get-tuple-element.12), channel_id=1, source_target_pairs={{0,124},{4,8},{8,4},{12,16},{16,12},{20,24},{24,20},{28,32},{32,28... | collective-permute-start | bytes 786440 | tf_op jit(solution)/shard_map/ppermute | solution.py:395
  11.1 10.3 %all-to-all-start = ((bf16[128,8,128]{2,1,0:T(8,128)(2,1)}), bf16[128,8,128]{2,1,0:T(8,128)(2,1)}, u32[]{:S(2)}, u32[]{:S(2)}) async-start(bf16[128,8,128]{2,1,0:T(8,128)(2,1)} %get-tuple-element.14), calls=%async_computation | async-start | bytes 524288 | tf_op jit(solution)/shard_map/all_to_all | solution.py:413
  21.4 0.0 collective-permute-done.inner
  21.4 0.0 collective-permute-done.1.outer
  21.4 0.0 collective-permute-done.3.from_high
  21.4 0.0 collective-permute-done.2.from_low
  21.5 5.3 %beside.1 = (bf16[64,16,256]{2,1,0:T(8,128)(2,1)}, bf16[64,16,256]{2,1,0:T(8,128)(2,1)}, s32[9,64]{1,0:T(8,128)}) custom-call(bf16[32,16,256]{2,1,0:T(8,128)(2,1)} %collective-permute-done.inner, bf16[32,16,256]{2,1,0:T(8,128)(2,1)} %collective-permute-done.1.outer, bf16[64,16,256]{2,1,0:T(8,128)(2,1)} %collective-permute-done.2.from_low, ...), custom_call_target="tpu_custom_call" | custom-call | tf_op jit(solution)/shard_map/beside/pallas_call | solution.py:207
  26.8 1.2 %collective-permute-start.4 = (bf16[64,16,256]{2,1,0:T(8,128)(2,1)}, bf16[64,16,256]{2,1,0:T(8,128)(2,1)S(1)}, u32[]{:S(2)}, u32[]{:S(2)}) collective-permute-start(bf16[64,16,256]{2,1,0:T(8,128)(2,1)} %get-tuple-element.15), channel_id=1, source_target_pairs={{0,4},{4,0},{8,12},{12,8},{16,20},{20,16},{24,28},{28,24},{32,36},... | collective-permute-start | bytes 1572872 | tf_op jit(solution)/shard_map/ppermute | solution.py:395
  28.0 0.8 %collective-permute-start.5 = (bf16[64,16,256]{2,1,0:T(8,128)(2,1)}, bf16[64,16,256]{2,1,0:T(8,128)(2,1)S(1)}, u32[]{:S(2)}, u32[]{:S(2)}) collective-permute-start(bf16[64,16,256]{2,1,0:T(8,128)(2,1)} %get-tuple-element.16), channel_id=1, source_target_pairs={{0,124},{4,8},{8,4},{12,16},{16,12},{20,24},{24,20},{28,32},{32,28... | collective-permute-start | bytes 1572872 | tf_op jit(solution)/shard_map/ppermute | solution.py:395
  28.7 3.7 %all-to-all-done.tops = bf16[128,8,128]{2,1,0:T(8,128)(2,1)} async-done(((bf16[128,8,128]{2,1,0:T(8,128)(2,1)}), bf16[128,8,128]{2,1,0:T(8,128)(2,1)}, u32[]{:S(2)}, u32[]{:S(2)}) %all-to-all-start) | async-done | bytes 262176 | tf_op jit(solution)/shard_map/all_to_all | solution.py:413
  32.4 7.3 %local.1 = bf16[64,16,256]{2,1,0:T(8,128)(2,1)} custom-call(s32[64]{0:T(128)} %parent.3, s32[8,8]{1,0:T(8,128)} %top_links.1, s32[8,16]{1,0:T(8,128)} %bitcast.4, s32[9,64]{1,0:T(8,128)} %get-tuple-element.13.codes, bf16[32,16,256]{2,1,0:T(8,128)(2,1)} %collective-permute-done.inner, bf16[32,16,256]{2,1,0:T(8,128)(2,1)} %collective-permute-done.1.outer, ...), custom_call_target="tpu_custom_call" | custom-call | flops 40000000000 | tf_op jit(solution)/shard_map/local/pallas_call | solution.py:356
  39.7 0.0 collective-permute-done.4
  39.8 0.0 collective-permute-done.5
  39.8 2.0 %add_convert_fusion = bf16[64,16,256]{2,1,0:T(8,128)(2,1)} fusion(bf16[64,16,256]{2,1,0:T(8,128)(2,1)S(1)} %collective-permute-done.5, bf16[64,16,256]{2,1,0:T(8,128)(2,1)S(1)} %collective-permute-done.4, bf16[64,16,256]{2,1,0:T(8,128)(2,1)} %local.1), kind=kLoop, calls=%fused_computation | loop fusion | flops 1572864 | bytes 2097152 | tf_op jit(solution)/shard_map/convert_element_type | solution.py:423
Async XLA Ops:
  0.0 21.4 %collective-permute-start.3 = (bf16[64,16,256]{2,1,0:T(8,128)(2,1)}, bf16[64,16,256]{2,1,0:T(8,128)(2,1)}, u32[]{:S(2)}, u32[]{:S(2)}) collective-permute-start(bf16[64,16,256]{2,1,0:T(8,128)(2,1)} %own_src.3), channel_id=1, source_target_pairs={{0,3},{1,0},{2,1},{3,2},{4,7},{5,4},{6,5},{7,6},{8,11},{9,8},{10,9... | collective-permute-start | bytes 1572872 | tf_op jit(solution)/shard_map/ppermute | solution.py:390
  3.3 18.1 %collective-permute-start.2 = (bf16[64,16,256]{2,1,0:T(8,128)(2,1)}, bf16[64,16,256]{2,1,0:T(8,128)(2,1)}, u32[]{:S(2)}, u32[]{:S(2)}) collective-permute-start(bf16[64,16,256]{2,1,0:T(8,128)(2,1)} %own_src.3), channel_id=1, source_target_pairs={{0,1},{1,2},{2,3},{3,0},{4,5},{5,6},{6,7},{7,4},{8,9},{9,10},{10,1... | collective-permute-start | bytes 1572872 | tf_op jit(solution)/shard_map/ppermute | solution.py:390
  8.4 13.0 %collective-permute-start = (bf16[32,16,256]{2,1,0:T(8,128)(2,1)}, bf16[32,16,256]{2,1,0:T(8,128)(2,1)}, u32[]{:S(2)}, u32[]{:S(2)}) collective-permute-start(bf16[32,16,256]{2,1,0:T(8,128)(2,1)} %get-tuple-element.11), channel_id=1, source_target_pairs={{0,4},{4,0},{8,12},{12,8},{16,20},{20,16},{24,28},{28,24},{32,36},... | collective-permute-start | bytes 786440 | tf_op jit(solution)/shard_map/ppermute | solution.py:395
  9.5 12.0 %collective-permute-start.1 = (bf16[32,16,256]{2,1,0:T(8,128)(2,1)}, bf16[32,16,256]{2,1,0:T(8,128)(2,1)}, u32[]{:S(2)}, u32[]{:S(2)}) collective-permute-start(bf16[32,16,256]{2,1,0:T(8,128)(2,1)} %get-tuple-element.12), channel_id=1, source_target_pairs={{0,124},{4,8},{8,4},{12,16},{16,12},{20,24},{24,20},{28,32},{32,28... | collective-permute-start | bytes 786440 | tf_op jit(solution)/shard_map/ppermute | solution.py:395
  11.1 21.3 %all-to-all-start = ((bf16[128,8,128]{2,1,0:T(8,128)(2,1)}), bf16[128,8,128]{2,1,0:T(8,128)(2,1)}, u32[]{:S(2)}, u32[]{:S(2)}) async-start(bf16[128,8,128]{2,1,0:T(8,128)(2,1)} %get-tuple-element.14), calls=%async_computation | async-start | bytes 524288 | tf_op jit(solution)/shard_map/all_to_all | solution.py:413
  26.8 13.0 %collective-permute-start.4 = (bf16[64,16,256]{2,1,0:T(8,128)(2,1)}, bf16[64,16,256]{2,1,0:T(8,128)(2,1)S(1)}, u32[]{:S(2)}, u32[]{:S(2)}) collective-permute-start(bf16[64,16,256]{2,1,0:T(8,128)(2,1)} %get-tuple-element.15), channel_id=1, source_target_pairs={{0,4},{4,0},{8,12},{12,8},{16,20},{20,16},{24,28},{28,24},{32,36},... | collective-permute-start | bytes 1572872 | tf_op jit(solution)/shard_map/ppermute | solution.py:395
  28.0 11.8 %collective-permute-start.5 = (bf16[64,16,256]{2,1,0:T(8,128)(2,1)}, bf16[64,16,256]{2,1,0:T(8,128)(2,1)S(1)}, u32[]{:S(2)}, u32[]{:S(2)}) collective-permute-start(bf16[64,16,256]{2,1,0:T(8,128)(2,1)} %get-tuple-element.16), channel_id=1, source_target_pairs={{0,124},{4,8},{8,4},{12,16},{16,12},{20,24},{24,20},{28,32},{32,28... | collective-permute-start | bytes 1572872 | tf_op jit(solution)/shard_map/ppermute | solution.py:395

commit v6 on v5

--- a/solution.py
+++ b/solution.py
@@ -78,7 +78,8 @@
         at = pl.ds(c * boxes, boxes)
         pairs += [(ref.at[at], buf.at[at]) for ref, buf in ((sources, src), (source_basis, basis), (up_leaf, lift))]
         if c == 0:
-            pairs += [(near_list, lists), (up_section, raise_)]
+            pairs.append((near_list, lists))
+    pairs.append((up_section, raise_))
     copies = started(pairs, sems)
     total[...] = jnp.zeros_like(total)
     to_inner[...] = jnp.zeros_like(to_inner)
@@ -86,7 +87,7 @@
     own = own_mask(rhs, rank)
     at_copy = 0
     for c in range(chunks):
-        many = 5 if c == 0 else 3
+        many = 4 if c == 0 else 3
         for copy in copies[at_copy : at_copy + many]:
             copy.wait()
         at_copy += many
@@ -108,6 +109,7 @@
             for one in range(4):
                 slot = parent[c * boxes + 4 * f + one] & (sections - 1)
                 total[slot] += x[one * rhs : (one + 1) * rhs]
+    copies[-1].wait()
     fours = sections // 4
     for four in range(fours):
         wide = jnp.concatenate([total[4 * four + one] for one in range(4)], axis=1)

time: 42.1 us -> 41.9 us (level)
  no operation moved by 1% of the time
where the time goes in v6:
time: 41.9 us; the launch traced here: 41.6 us
  starting transfers between devices  18.3 us (44%)
  Pallas kernels  17.6 us (42%)
  waiting for transfers between devices  3.67 us (9%)
  other arithmetic  2.04 us (5%)
    all_to_all x1, starting transfers between devices, shards(): tops = lax.all_to_all(sent, ('leaf', 'slab'), 0, 0, tiled=True)  10.3 us
    pallas_call x1, Pallas kernels, local_call(): pl.pallas_call(local_kernel, in_specs=[SMEM] * 4 + [HBM] * 12, out_specs=...  7.34 us
    pallas_call x1, Pallas kernels, beside_call(): pl.pallas_call(beside_kernel, in_specs=[HBM] * 7, out_specs=[VMEM] * 3, o...  5.28 us
    pallas_call x1, Pallas kernels, moments_call(): pl.pallas_call(moments_kernel, in_specs=[SMEM, HBM, HBM, HBM, HBM, HBM],...  4.94 us
    ppermute x4, starting transfers between devices, swapped(): lax.ppermute(x, 'leaf', [(i, (i + (1 if i % 2 == first else -1)) % count)...  4.63 us
    all_to_all x1, waiting for transfers between devices, shards(): tops = lax.all_to_all(sent, ('leaf', 'slab'), 0, 0, tiled=True)  3.66 us
    ppermute x2, starting transfers between devices, shifted(): lax.ppermute(x, axis, [(i, (i + step) % count) for i in range(count)])  3.31 us
    convert_element_type x1, other arithmetic, shards(): (local.astype(F32) + near_inner.astype(F32) + near_outer.astype(F32)).ast...  2.04 us
  transfers between devices with their start and end apart: 7, of which 1 were waited for; matrix products, arithmetic and copies ran while one was open for 0% of the time, Pallas kernels for 42%

profile of v6, /device:TPU:1, one launch (start us, length us, event | category | flops | bytes accessed | tf_op | source)
XLA Modules:
  0.0 41.6 jit_solution(2863394004794579957)
XLA Ops:
  0.0 3.3 %collective-permute-start.3 = (bf16[64,16,256]{2,1,0:T(8,128)(2,1)}, bf16[64,16,256]{2,1,0:T(8,128)(2,1)}, u32[]{:S(2)}, u32[]{:S(2)}) collective-permute-start(bf16[64,16,256]{2,1,0:T(8,128)(2,1)} %own_src.3), channel_id=1, source_target_pairs={{0,3},{1,0},{2,1},{3,2},{4,7},{5,4},{6,5},{7,6},{8,11},{9,8},{10,9... | collective-permute-start | bytes 1572872 | tf_op jit(solution)/shard_map/ppermute | solution.py:392
  3.3 0.0 collective-permute-start.2
  3.3 4.9 %moments.1 = (bf16[32,16,256]{2,1,0:T(8,128)(2,1)}, bf16[32,16,256]{2,1,0:T(8,128)(2,1)}, bf16[128,8,128]{2,1,0:T(8,128)(2,1)}) custom-call(s32[64]{0:T(128)} %parent.3, bf16[64,16,256]{2,1,0:T(8,128)(2,1)} %own_src.3, bf16[64,64,256]{2,1,0:T(8,128)(2,1)} %source_basis.1, f32[64,64,64]{2,1,0:T(8,128)} %up_leaf.1, f32[16,64,64]{2,1,0:T(8,128)} %up_section.1, ...), custom_call_target="tpu_custom_call" | custom-call | tf_op jit(solution)/shard_map/moments/pallas_call | solution.py:137
  8.3 1.0 %collective-permute-start = (bf16[32,16,256]{2,1,0:T(8,128)(2,1)}, bf16[32,16,256]{2,1,0:T(8,128)(2,1)}, u32[]{:S(2)}, u32[]{:S(2)}) collective-permute-start(bf16[32,16,256]{2,1,0:T(8,128)(2,1)} %get-tuple-element.11), channel_id=1, source_target_pairs={{0,4},{4,0},{8,12},{12,8},{16,20},{20,16},{24,28},{28,24},{32,36},... | collective-permute-start | bytes 786440 | tf_op jit(solution)/shard_map/ppermute | solution.py:397
  9.3 1.6 %collective-permute-start.1 = (bf16[32,16,256]{2,1,0:T(8,128)(2,1)}, bf16[32,16,256]{2,1,0:T(8,128)(2,1)}, u32[]{:S(2)}, u32[]{:S(2)}) collective-permute-start(bf16[32,16,256]{2,1,0:T(8,128)(2,1)} %get-tuple-element.12), channel_id=1, source_target_pairs={{0,124},{4,8},{8,4},{12,16},{16,12},{20,24},{24,20},{28,32},{32,28... | collective-permute-start | bytes 786440 | tf_op jit(solution)/shard_map/ppermute | solution.py:397
  10.9 10.3 %all-to-all-start = ((bf16[128,8,128]{2,1,0:T(8,128)(2,1)}), bf16[128,8,128]{2,1,0:T(8,128)(2,1)}, u32[]{:S(2)}, u32[]{:S(2)}) async-start(bf16[128,8,128]{2,1,0:T(8,128)(2,1)} %get-tuple-element.14), calls=%async_computation | async-start | bytes 524288 | tf_op jit(solution)/shard_map/all_to_all | solution.py:415
  21.2 0.0 collective-permute-done.inner
  21.3 0.0 collective-permute-done.1.outer
  21.3 0.0 collective-permute-done.3.from_high
  21.3 0.0 collective-permute-done.2.from_low
  21.3 5.3 %beside.1 = (bf16[64,16,256]{2,1,0:T(8,128)(2,1)}, bf16[64,16,256]{2,1,0:T(8,128)(2,1)}, s32[9,64]{1,0:T(8,128)}) custom-call(bf16[32,16,256]{2,1,0:T(8,128)(2,1)} %collective-permute-done.inner, bf16[32,16,256]{2,1,0:T(8,128)(2,1)} %collective-permute-done.1.outer, bf16[64,16,256]{2,1,0:T(8,128)(2,1)} %collective-permute-done.2.from_low, ...), custom_call_target="tpu_custom_call" | custom-call | tf_op jit(solution)/shard_map/beside/pallas_call | solution.py:209
  26.6 1.2 %collective-permute-start.4 = (bf16[64,16,256]{2,1,0:T(8,128)(2,1)}, bf16[64,16,256]{2,1,0:T(8,128)(2,1)S(1)}, u32[]{:S(2)}, u32[]{:S(2)}) collective-permute-start(bf16[64,16,256]{2,1,0:T(8,128)(2,1)} %get-tuple-element.15), channel_id=1, source_target_pairs={{0,4},{4,0},{8,12},{12,8},{16,20},{20,16},{24,28},{28,24},{32,36},... | collective-permute-start | bytes 1572872 | tf_op jit(solution)/shard_map/ppermute | solution.py:397
  27.8 0.8 %collective-permute-start.5 = (bf16[64,16,256]{2,1,0:T(8,128)(2,1)}, bf16[64,16,256]{2,1,0:T(8,128)(2,1)S(1)}, u32[]{:S(2)}, u32[]{:S(2)}) collective-permute-start(bf16[64,16,256]{2,1,0:T(8,128)(2,1)} %get-tuple-element.16), channel_id=1, source_target_pairs={{0,124},{4,8},{8,4},{12,16},{16,12},{20,24},{24,20},{28,32},{32,28... | collective-permute-start | bytes 1572872 | tf_op jit(solution)/shard_map/ppermute | solution.py:397
  28.6 3.7 %all-to-all-done.tops = bf16[128,8,128]{2,1,0:T(8,128)(2,1)} async-done(((bf16[128,8,128]{2,1,0:T(8,128)(2,1)}), bf16[128,8,128]{2,1,0:T(8,128)(2,1)}, u32[]{:S(2)}, u32[]{:S(2)}) %all-to-all-start) | async-done | bytes 262176 | tf_op jit(solution)/shard_map/all_to_all | solution.py:415
  32.2 7.3 %local.1 = bf16[64,16,256]{2,1,0:T(8,128)(2,1)} custom-call(s32[64]{0:T(128)} %parent.3, s32[8,8]{1,0:T(8,128)} %top_links.1, s32[8,16]{1,0:T(8,128)} %bitcast.4, s32[9,64]{1,0:T(8,128)} %get-tuple-element.13.codes, bf16[32,16,256]{2,1,0:T(8,128)(2,1)} %collective-permute-done.inner, bf16[32,16,256]{2,1,0:T(8,128)(2,1)} %collective-permute-done.1.outer, ...), custom_call_target="tpu_custom_call" | custom-call | flops 40000000000 | tf_op jit(solution)/shard_map/local/pallas_call | solution.py:358
  39.6 0.0 collective-permute-done.4
  39.6 0.0 collective-permute-done.5
  39.6 2.0 %add_convert_fusion = bf16[64,16,256]{2,1,0:T(8,128)(2,1)} fusion(bf16[64,16,256]{2,1,0:T(8,128)(2,1)S(1)} %collective-permute-done.5, bf16[64,16,256]{2,1,0:T(8,128)(2,1)S(1)} %collective-permute-done.4, bf16[64,16,256]{2,1,0:T(8,128)(2,1)} %local.1), kind=kLoop, calls=%fused_computation | loop fusion | flops 1572864 | bytes 2097152 | tf_op jit(solution)/shard_map/convert_element_type | solution.py:425
Async XLA Ops:
  0.0 21.3 %collective-permute-start.3 = (bf16[64,16,256]{2,1,0:T(8,128)(2,1)}, bf16[64,16,256]{2,1,0:T(8,128)(2,1)}, u32[]{:S(2)}, u32[]{:S(2)}) collective-permute-start(bf16[64,16,256]{2,1,0:T(8,128)(2,1)} %own_src.3), channel_id=1, source_target_pairs={{0,3},{1,0},{2,1},{3,2},{4,7},{5,4},{6,5},{7,6},{8,11},{9,8},{10,9... | collective-permute-start | bytes 1572872 | tf_op jit(solution)/shard_map/ppermute | solution.py:392
  3.3 18.0 %collective-permute-start.2 = (bf16[64,16,256]{2,1,0:T(8,128)(2,1)}, bf16[64,16,256]{2,1,0:T(8,128)(2,1)}, u32[]{:S(2)}, u32[]{:S(2)}) collective-permute-start(bf16[64,16,256]{2,1,0:T(8,128)(2,1)} %own_src.3), channel_id=1, source_target_pairs={{0,1},{1,2},{2,3},{3,0},{4,5},{5,6},{6,7},{7,4},{8,9},{9,10},{10,1... | collective-permute-start | bytes 1572872 | tf_op jit(solution)/shard_map/ppermute | solution.py:392
  8.3 13.0 %collective-permute-start = (bf16[32,16,256]{2,1,0:T(8,128)(2,1)}, bf16[32,16,256]{2,1,0:T(8,128)(2,1)}, u32[]{:S(2)}, u32[]{:S(2)}) collective-permute-start(bf16[32,16,256]{2,1,0:T(8,128)(2,1)} %get-tuple-element.11), channel_id=1, source_target_pairs={{0,4},{4,0},{8,12},{12,8},{16,20},{20,16},{24,28},{28,24},{32,36},... | collective-permute-start | bytes 786440 | tf_op jit(solution)/shard_map/ppermute | solution.py:397
  9.3 12.0 %collective-permute-start.1 = (bf16[32,16,256]{2,1,0:T(8,128)(2,1)}, bf16[32,16,256]{2,1,0:T(8,128)(2,1)}, u32[]{:S(2)}, u32[]{:S(2)}) collective-permute-start(bf16[32,16,256]{2,1,0:T(8,128)(2,1)} %get-tuple-element.12), channel_id=1, source_target_pairs={{0,124},{4,8},{8,4},{12,16},{16,12},{20,24},{24,20},{28,32},{32,28... | collective-permute-start | bytes 786440 | tf_op jit(solution)/shard_map/ppermute | solution.py:397
  10.9 21.3 %all-to-all-start = ((bf16[128,8,128]{2,1,0:T(8,128)(2,1)}), bf16[128,8,128]{2,1,0:T(8,128)(2,1)}, u32[]{:S(2)}, u32[]{:S(2)}) async-start(bf16[128,8,128]{2,1,0:T(8,128)(2,1)} %get-tuple-element.14), calls=%async_computation | async-start | bytes 524288 | tf_op jit(solution)/shard_map/all_to_all | solution.py:415
  26.6 13.0 %collective-permute-start.4 = (bf16[64,16,256]{2,1,0:T(8,128)(2,1)}, bf16[64,16,256]{2,1,0:T(8,128)(2,1)S(1)}, u32[]{:S(2)}, u32[]{:S(2)}) collective-permute-start(bf16[64,16,256]{2,1,0:T(8,128)(2,1)} %get-tuple-element.15), channel_id=1, source_target_pairs={{0,4},{4,0},{8,12},{12,8},{16,20},{20,16},{24,28},{28,24},{32,36},... | collective-permute-start | bytes 1572872 | tf_op jit(solution)/shard_map/ppermute | solution.py:397
  27.8 11.8 %collective-permute-start.5 = (bf16[64,16,256]{2,1,0:T(8,128)(2,1)}, bf16[64,16,256]{2,1,0:T(8,128)(2,1)S(1)}, u32[]{:S(2)}, u32[]{:S(2)}) collective-permute-start(bf16[64,16,256]{2,1,0:T(8,128)(2,1)} %get-tuple-element.16), channel_id=1, source_target_pairs={{0,124},{4,8},{8,4},{12,16},{16,12},{20,24},{24,20},{28,32},{32,28... | collective-permute-start | bytes 1572872 | tf_op jit(solution)/shard_map/ppermute | solution.py:397
